TPU v7x, 32 devices: a whole 2x2x4 slice. The times are simulated.
32 devices in a mesh: cell: 4 (over z), level: 4 (over y, x), rep: 2 (over core).
Axes of the slice: x: 2, y: 2, z: 4, core: 2. Of those that a mesh axis runs over, the one named last changes fastest.
Arguments:
- resident_pos: float32 [2, 32, 128, 512], P(None, 'rep', 'level', 'cell'), may hold values from -0.5 to 0.5
- resident_strength: float32 [32, 128, 512], P('rep', 'level', 'cell'), may hold values from -0.51 to 0.51
- mover_pos: float32 [2, 2, 4, 16384], P(None, 'rep', 'level', 'cell'), may hold values from -0.5 to 0.5
- mover_strength: float32 [2, 4, 16384], P('rep', 'level', 'cell'), may hold values from -0.51 to 0.51
- mover_owner: int32 [2, 4, 16384], P('rep', 'level', 'cell'), may hold values from 0 to 3, as said below
- mover_leaf: int32 [2, 4, 16384], P('rep', 'level', 'cell'), may hold values from 0 to 4095, as said below
- mover_slot: int32 [2, 4, 16384], P('rep', 'level', 'cell'), may hold values from 0 to 15
Outputs:
- velocity: float32 [2, 32, 128, 512], P(None, 'rep', 'level', 'cell')
Inputs may be any that keep to these rules, and one draw needn't show every extreme that they name: `mover_owner`: for one rep and level index, the 4096 movers of one device name one owner at most 1024 times, and one owner is named exactly 1024 times by every device. `mover_leaf`: leaf key y * 128 + x inside the owner's domain; for one rep and level index no (owner, leaf, slot) triple appears twice.
All inputs are finite; a program needn't handle non-finite values.
Results may differ from a plain program's by a relative error of at most 0.0003.
Values sent between devices are 32-bit elements; how exact they have to be, the bound alone decides.
A program may use at most 192 MiB of HBM per device.

v0:
```python
import math

import jax
import jax.numpy as jnp
import numpy as np
from jax import lax
from jax.sharding import PartitionSpec as P

ORDER = 10
HALO_LEVELS = 4
CAP = 1024


precise = lax.Precision.HIGHEST
blob_square = 0.09


def with_halo(shard, sides, width):
    for axis, dim in sides:
        devices, length = (lax.axis_size(axis), shard.shape[dim])
        up = [(i, (i + 1) % devices) for i in range(devices - 1)]
        down = [(j, i) for i, j in up]
        last = lax.slice_in_dim(shard, length - width, length, axis=dim)
        first = lax.slice_in_dim(shard, 0, width, axis=dim)
        before = lax.ppermute(last, axis, up)
        after = lax.ppermute(first, axis, down)
        shard = jnp.concatenate([before, shard, after], axis=dim)
    return shard


def real_form(matrix):
    top_rows = np.concatenate([matrix.real, -matrix.imag], axis=1)
    low_rows = np.concatenate([matrix.imag, matrix.real], axis=1)
    return np.concatenate([top_rows, low_rows], axis=0)


def child_offset(parity_x, parity_y):
    return complex((parity_x - 0.5) / 2.0, (parity_y - 0.5) / 2.0)


def upward_table(parity_x, parity_y):
    offset = child_offset(parity_x, parity_y)
    matrix = np.zeros((ORDER, ORDER), complex)
    for k in range(ORDER):
        for m in range(k + 1):
            matrix[k, m] = math.comb(k, m) * 0.5**m * offset ** (k - m)
    return real_form(matrix)


def downward_table(parity_x, parity_y):
    offset = child_offset(parity_x, parity_y)
    matrix = np.zeros((ORDER, ORDER), complex)
    for m in range(ORDER):
        for l in range(m, ORDER):
            matrix[m, l] = 0.5 ** (m + 1) * math.comb(l, m) * offset ** (l - m)
    return real_form(matrix)


def far_table(step_x, step_y):
    distance = complex(step_x, step_y)
    matrix = np.zeros((ORDER, ORDER), complex)
    for l in range(ORDER):
        for k in range(ORDER):
            matrix[l, k] = (-1) ** (k + 1) * math.comb(k + l, l) * distance ** (-(k + l + 1))
    return real_form(matrix)


def apply_matrix(matrix, level_field):
    return jnp.einsum(
        "ij,jyx->iyx", jnp.asarray(matrix, dtype=jnp.float32), level_field, precision=precise
    )


def upward(level_field):
    summed = None
    for parity_y in (0, 1):
        for parity_x in (0, 1):
            product = apply_matrix(
                upward_table(parity_x, parity_y), level_field[:, parity_y::2, parity_x::2]
            )
            summed = product if summed is None else summed + product
    return summed


def downward(parent):
    channels, cells_y, cells_x = parent.shape
    pieces = jnp.stack(
        [
            jnp.stack(
                [apply_matrix(downward_table(parity_x, parity_y), parent) for parity_x in (0, 1)]
            )
            for parity_y in (0, 1)
        ]
    )
    return pieces.transpose(2, 3, 0, 4, 1).reshape(channels, 2 * cells_y, 2 * cells_x)


def grouped_far(padded, margin_cells, cells_y, cells_x):
    classes = []
    for parity_y in (0, 1):
        row_parts = []
        for parity_x in (0, 1):
            pieces = []
            blocks = []
            for step_y in range(-2 - parity_y, 4 - parity_y):
                for step_x in range(-2 - parity_x, 4 - parity_x):
                    if max(abs(step_x), abs(step_y)) <= 1:
                        continue
                    first_y = margin_cells + parity_y + step_y
                    first_x = margin_cells + parity_x + step_x
                    pieces.append(
                        padded[:, first_y : first_y + cells_y : 2, first_x : first_x + cells_x : 2]
                    )
                    blocks.append(far_table(step_x, step_y))
            row_parts.append(
                apply_matrix(np.concatenate(blocks, axis=1), jnp.concatenate(pieces, axis=0))
            )
        classes.append(jnp.stack(row_parts))
    joined = jnp.stack(classes)
    return joined.transpose(2, 3, 0, 4, 1).reshape(joined.shape[2], cells_y, cells_x)


def top_far(level_field):
    channels, cells_y, cells_x = level_field.shape
    reach_y = cells_y - 1
    reach_x = cells_x - 1
    padded = jnp.pad(level_field, ((0, 0), (reach_y, reach_y), (reach_x, reach_x)))
    summed = jnp.zeros(level_field.shape, jnp.float32)
    for step_y in range(-reach_y, reach_y + 1):
        for step_x in range(-reach_x, reach_x + 1):
            if max(abs(step_x), abs(step_y)) <= 1:
                continue
            source = padded[
                :,
                reach_y + step_y : reach_y + step_y + cells_y,
                reach_x + step_x : reach_x + step_x + cells_x,
            ]
            summed = summed + apply_matrix(far_table(step_x, step_y), source)
    return summed


def moments(pos_x, pos_y, strength):
    real_power = jnp.ones_like(pos_x)
    imag_power = jnp.zeros_like(pos_x)
    real_rows = []
    imag_rows = []
    for k in range(ORDER):
        real_rows.append(jnp.sum(strength * real_power, axis=0))
        imag_rows.append(jnp.sum(strength * imag_power, axis=0))
        real_power, imag_power = (
            real_power * pos_x - imag_power * pos_y,
            real_power * pos_y + imag_power * pos_x,
        )
    return jnp.stack(real_rows + imag_rows)


def evaluate(local_field, pos_x, pos_y):
    real_acc = jnp.broadcast_to(local_field[ORDER - 1], pos_x.shape)
    imag_acc = jnp.broadcast_to(local_field[2 * ORDER - 1], pos_x.shape)
    for l in range(ORDER - 2, -1, -1):
        real_acc, imag_acc = (
            real_acc * pos_x - imag_acc * pos_y + local_field[l],
            real_acc * pos_y + imag_acc * pos_x + local_field[ORDER + l],
        )
    return (real_acc, imag_acc)


def framing(level_field):
    return with_halo(level_field, (("cell", 2), ("level", 1)), 3)


def local(
    resident_pos, resident_strength, mover_pos, mover_strength, mover_owner, mover_leaf, mover_slot
):
    cell_count = lax.axis_size("cell")
    level_count = lax.axis_size("level")
    half_slots, cells_y, cells_x = resident_strength.shape
    leaves = cells_y * cells_x
    owner_cell = mover_owner.reshape(-1)
    address = mover_slot.reshape(-1) * leaves + mover_leaf.reshape(-1)
    peer_ids = jnp.arange(cell_count, dtype=jnp.int32)
    onehot = (owner_cell[:, None] == peer_ids[None, :]).astype(jnp.int32)
    rank_in_owner = jnp.sum(jnp.cumsum(onehot, axis=0) * onehot, axis=1) - 1
    values = jnp.concatenate([mover_pos.reshape(2, -1), mover_strength.reshape(1, -1)])
    outgoing = (
        jnp.zeros((3, cell_count, CAP), jnp.float32).at[:, owner_cell, rank_in_owner].set(values)
    )
    addresses = (
        jnp.full((1, cell_count, CAP), half_slots * leaves, jnp.int32)
        .at[0, owner_cell, rank_in_owner]
        .set(address)
    )
    arrived, arrived_at = (
        lax.all_to_all(outgoing, "cell", split_axis=1, concat_axis=1, tiled=True),
        lax.all_to_all(addresses, "cell", split_axis=1, concat_axis=1, tiled=True),
    )
    resident = jnp.concatenate([resident_pos.reshape(2, -1), resident_strength.reshape(1, -1)])
    settled = resident.at[:, arrived_at.reshape(-1)].set(arrived.reshape(3, -1), mode="drop")
    particles = settled.reshape(3, half_slots, cells_y, cells_x)
    whole = lax.all_gather(particles, "rep", axis=1, tiled=True)
    framed = with_halo(whole, (("cell", 3), ("level", 2)), 1)
    whole_inner = framed[:, :, 1:-1, 1:-1]
    level_zero = moments(whole_inner[0], whole_inner[1], whole_inner[2])
    owned = [level_zero]
    for k in range(HALO_LEVELS):
        owned.append(upward(owned[-1]))
    framed_levels = [framing(owned[k]) for k in range(HALO_LEVELS)]
    coarse_own = owned[HALO_LEVELS]
    channels, coarse_y, coarse_x = coarse_own.shape
    collected = lax.all_gather(coarse_own[None], ("cell", "level"), axis=0, tiled=True)
    coarse_grid = collected.reshape(cell_count, level_count, channels, coarse_y, coarse_x)
    coarse_grid = coarse_grid.transpose(2, 1, 3, 0, 4).reshape(
        channels, level_count * coarse_y, cell_count * coarse_x
    )
    coarse_fields = [coarse_grid]
    top_level = min(cell_count * cells_x, level_count * cells_y).bit_length() - 1
    for k in range(HALO_LEVELS + 1, top_level + 1):
        coarse_fields.append(upward(coarse_fields[-1]))
    local_field = top_far(coarse_fields[-1])
    for index in range(len(coarse_fields) - 2, -1, -1):
        level_field = coarse_fields[index]
        padded = jnp.pad(level_field, ((0, 0), (3, 3), (3, 3)))
        local_field = grouped_far(padded, 3, level_field.shape[1], level_field.shape[2]) + downward(
            local_field
        )
    local_field = lax.dynamic_slice(
        local_field,
        (0, lax.axis_index("level") * coarse_y, lax.axis_index("cell") * coarse_x),
        (channels, coarse_y, coarse_x),
    )
    for k in range(HALO_LEVELS - 1, -1, -1):
        level_field = owned[k]
        local_field = grouped_far(
            framed_levels[k], 3, level_field.shape[1], level_field.shape[2]
        ) + downward(local_field)
    far_real, far_imag = evaluate(local_field, particles[0], particles[1])
    slot_count = framed.shape[1]
    slot_base = lax.axis_index("rep") * half_slots
    target_slots = slot_base + jnp.arange(half_slots, dtype=jnp.int32)
    keep_mask = (target_slots[:, None] != jnp.arange(slot_count, dtype=jnp.int32)[None, :]).astype(
        jnp.float32
    )[:, :, None, None]
    band_rows = 8

    def near_band(row_start):
        target = lax.dynamic_slice_in_dim(particles, row_start, band_rows, 2)
        real_sum = jnp.zeros((half_slots, band_rows, cells_x), jnp.float32)
        imag_sum = jnp.zeros((half_slots, band_rows, cells_x), jnp.float32)
        for step_y in (-1, 0, 1):
            row_band = lax.dynamic_slice_in_dim(framed, row_start + 1 + step_y, band_rows, 2)
            for step_x in (-1, 0, 1):
                source = row_band[:, :, :, 1 + step_x : 1 + step_x + cells_x]
                gap_x = target[0][:, None] - source[0][None] - step_x
                gap_y = target[1][:, None] - source[1][None] - step_y
                weight = source[2][None] / (gap_x * gap_x + gap_y * gap_y + blob_square)
                if step_x == 0 and step_y == 0:
                    weight = weight * keep_mask
                real_sum = real_sum + jnp.sum(weight * gap_x, axis=1)
                imag_sum = imag_sum - jnp.sum(weight * gap_y, axis=1)
        return jnp.stack([real_sum, imag_sum])

    starts = jnp.arange(0, cells_y, band_rows, dtype=jnp.int32)
    bands = lax.map(near_band, starts)
    near = bands.transpose(1, 2, 0, 3, 4).reshape(2, half_slots, cells_y, cells_x)
    real_part = near[0] + far_real
    imag_part = near[1] + far_imag
    return jnp.stack([imag_part, real_part]) / (2.0 * math.pi)


def solution(mesh):
    return jax.shard_map(
        local,
        mesh=mesh,
        in_specs=(
            P(None, "rep", "level", "cell"),
            P("rep", "level", "cell"),
            P(None, "rep", "level", "cell"),
            P("rep", "level", "cell"),
            P("rep", "level", "cell"),
            P("rep", "level", "cell"),
            P("rep", "level", "cell"),
        ),
        out_specs=P(None, "rep", "level", "cell"),
        check_vma=False,
    )
```

profile of v0, /device:TPU:0, one launch (start us, length us, event | category | flops | bytes accessed | tf_op | source)
XLA Modules:
  0.0 961.5 jit_solution(14797197037400876921)
XLA Ops:
  12.9 16.1 %scatter_custom_fusion.1 = s32[4096]{0:T(1024)} fusion(s32[4096]{0:T(1024)S(1)} %broadcast_select_fusion.1, s32[4096]{0:T(1024)S(1)} %bitcast.946, s32[]{:T(128)} %constant.170.clone.1), kind=kCustom, calls=%fused_computation.367 | custom fusion | bytes 16388
  29.0 6.3 all-to-all-start
  42.7 12.3 %scatter_custom_fusion.2 = f32[3,4096]{0,1:T(8,128)} fusion(s32[4096]{0:T(1024)S(1)} %broadcast_select_fusion, f32[4096,3]{1,0:T(8,128)} %copy.1486, f32[]{:T(128)} %constant.168.clone.1), kind=kCustom, calls=%fused_computation.176 | custom fusion | bytes 49664
  57.9 16.0 %copy.1488 = f32[3,65536]{0,1:T(8,128)} copy(f32[3,65536]{1,0:T(4,128)S(1)} %pad_maximum_fusion.1) | data formatting | bytes 1572864 | tf_op jit(solution)/shard_map/concatenate | solution.py:197
  79.1 5.7 all-to-all-done.1
  86.7 32.6 %scatter_fusion = f32[3,65536]{0,1:T(8,128)} fusion(f32[3,65536]{0,1:T(8,128)} %copy.1488, s32[4096]{0:T(1024)S(1)} %bitcast.941, f32[4096,3]{1,0:T(8,128)} %copy.1489), kind=kCustom, calls=%fused_computation | custom fusion | bytes 163840 | tf_op jit(solution)/shard_map/scatter | solution.py:198
  119.4 20.2 %copy.1851 = f32[3,16,32,128]{3,2,1,0:T(8,128)} copy(f32[3,16,32,128]{0,3,2,1:T(8,128)} %bitcast.873) | data formatting | bytes 1572864 | tf_op jit(solution)/shard_map/reshape | solution.py:199
  139.6 35.7 %slice_reduce_fusion.1 = (f32[65536]{0:T(1024)}, f32[65536]{0:T(1024)}) fusion(f32[3,65536]{0,1:T(8,128)} %scatter_fusion), kind=kLoop, calls=%fused_computation.102 | loop fusion | bytes 1048576 | tf_op jit(solution)/shard_map/slice | solution.py:236
  205.5 40.2 %all-gather = f32[320,2,8]{2,1,0:T(2,128)S(1)} all-gather(f32[20,2,8]{2,1,0:T(2,128)S(1)} %copy.1796), channel_id=2, replica_groups=mesh['cell'=4,'level'=4,'rep'=2] {'cell','level'}, dimensions={0}, use_global_device_ids=true | all-gather | bytes 21760 | tf_op jit(solution)/shard_map/all_gather | solution.py:210
  296.6 5.2 collective-permute-start.8
  356.4 5.2 collective-permute-start.14
  373.5 5.1 collective-permute-start.10
  401.2 5.2 collective-permute-start.6
  459.7 5.2 collective-permute-start.2
  746.3 9.6 concatenate.134
  755.9 9.6 concatenate.135
  765.5 9.6 concatenate.136
  775.0 9.9 %concatenate.137 = f32[540,16,64]{0,2,1:T(8,128)} concatenate(f32[20,16,64]{0,2,1:T(8,128)S(1)} %copy.1873, f32[20,16,64]{0,2,1:T(8,128)} %copy.1874, f32[20,16,64]{0,2,1:T(8,128)} %copy.1875, f32[20,16,64]{0,2,1:T(8,128)} %copy.1876, f32[20,16,64]{0,2,1:T(8,128)} %copy.1877, f32[20,16,64]{0,2,1:T(8,128)} %copy.1878, f32[20,16,64]{0,2,1:T(8,128)} %copy.1879, ...), dimensions={0} | concatenate | bytes 4423680 | tf_op jit(solution)/shard_map/concatenate | solution.py:116
  785.0 5.7 convolution_bitcast_fusion.7
  844.3 105.3 %while.16 = (s32[]{:T(128)}, f32[4,2,16,8,128]{4,3,2,1,0:T(8,128)}, s32[4]{0:T(128)}, f32[3,32,34,130]{3,2,1,0:T(8,128)}, f32[3,16,32,128]{3,2,1,0:T(8,128)}, /*...) while((s32[]{:T(128)}, f32[4,2,16,8,128]{4,3,2,1,0:T(8,128)}, ...), condition=%wide.region_25.26_spmd.clone, body=%wide.region_6.25_spmd.clone.sunk | while | flops 58737680 | bytes 14422976 | solution.py:263
  850.4 7.3 dynamic-slice_bitcast_fusion.31
  876.8 7.1 dynamic-slice_bitcast_fusion.31
  903.0 7.7 dynamic-slice_bitcast_fusion.31
  929.8 6.9 dynamic-slice_bitcast_fusion.31
  (883 shorter events, 635.2 us)
Async XLA Ops:
  29.0 44.9 %all-to-all-start = ((s32[1,4,1024]{2,0,1:T(1,128)}), s32[1,4,1024]{2,0,1:T(1,128)S(1)}, u32[]{:S(2)}, u32[]{:S(2)}) async-start(s32[1,4,1024]{2,0,1:T(1,128)} %bitcast.8), calls=%async_computation | async-start | bytes 32768 | tf_op jit(solution)/shard_map/all_to_all | solution.py:195
  73.9 10.8 %all-to-all-start.1 = ((f32[3,4,1024]{2,0,1:T(4,128)}), f32[3,4,1024]{2,0,1:T(4,128)S(1)}, u32[]{:S(2)}, u32[]{:S(2)}) async-start(f32[3,4,1024]{2,0,1:T(4,128)} %copy.1487), calls=%async_computation.1 | async-start | bytes 131072 | tf_op jit(solution)/shard_map/all_to_all | solution.py:194
  79.0 96.3 %all-gather.3.cloned.1.call-start = ((), (), s32[]{:S(2)}) async-start(), calls=%async_computation.2 | async-start | bytes 2359296 | tf_op jit(solution)/shard_map/all_gather | solution.py:200
  193.5 145.1 %copy-start.9 = (f32[20,16,64]{2,0,1:T(8,128)}, f32[20,16,64]{2,0,1:T(8,128)S(1)}, u32[]{:S(2)}) copy-start(f32[20,16,64]{2,0,1:T(8,128)S(1)} %fusion.25) | copy-start | bytes 245764
  288.2 22.4 %collective-permute-start.16 = (f32[20,4,3]{0,2,1:T(4,128)S(1)}, f32[20,4,3]{0,2,1:T(4,128)S(1)}, u32[]{:S(2)}, u32[]{:S(2)}) collective-permute-start(f32[20,4,3]{0,2,1:T(4,128)S(1)} %get-tuple-element.364), channel_id=1, source_target_pairs={{0,8},{8,16},{16,24},{1,9},{9,17},{17,25},{2,10},{10,18},{18,26},{... | collective-permute-start | bytes 2888 | tf_op jit(solution)/shard_map/ppermute | solution.py:25
  289.5 22.4 %collective-permute-start.17 = (f32[20,4,3]{0,2,1:T(4,128)S(1)}, f32[20,4,3]{0,2,1:T(4,128)S(1)}, u32[]{:S(2)}, u32[]{:S(2)}) collective-permute-start(f32[20,4,3]{0,2,1:T(4,128)S(1)} %get-tuple-element.365), channel_id=1, source_target_pairs={{8,0},{16,8},{24,16},{9,1},{17,9},{25,17},{10,2},{18,10},{26,18},{... | collective-permute-start | bytes 2888 | tf_op jit(solution)/shard_map/ppermute | solution.py:26
  290.8 27.7 %collective-permute-start.12 = (f32[20,8,3]{2,0,1:T(8,128)S(1)}, f32[20,8,3]{2,0,1:T(8,128)S(1)}, u32[]{:S(2)}, u32[]{:S(2)}) collective-permute-start(f32[20,8,3]{2,0,1:T(8,128)S(1)} %get-tuple-element.360), channel_id=1, source_target_pairs={{0,8},{8,16},{16,24},{1,9},{9,17},{17,25},{2,10},{10,18},{18,26},{... | collective-permute-start | bytes 5768 | tf_op jit(solution)/shard_map/ppermute | solution.py:25
  295.3 24.5 %collective-permute-start.13 = (f32[20,8,3]{2,0,1:T(8,128)}, f32[20,8,3]{2,0,1:T(8,128)S(1)}, u32[]{:S(2)}, u32[]{:S(2)}) collective-permute-start(f32[20,8,3]{2,0,1:T(8,128)} %get-tuple-element.361), channel_id=1, source_target_pairs={{8,0},{16,8},{24,16},{9,1},{17,9},{25,17},{10,2},{18,10},{26,18},{... | collective-permute-start | bytes 5768 | tf_op jit(solution)/shard_map/ppermute | solution.py:26
  296.6 39.2 %collective-permute-start.8 = (f32[20,16,3]{2,0,1:T(8,128)}, f32[20,16,3]{2,0,1:T(8,128)}, u32[]{:S(2)}, u32[]{:S(2)}) collective-permute-start(f32[20,16,3]{2,0,1:T(8,128)} %get-tuple-element.356), channel_id=1, source_target_pairs={{0,8},{8,16},{16,24},{1,9},{9,17},{17,25},{2,10},{10,18},{18,26},{... | collective-permute-start | bytes 11528 | tf_op jit(solution)/shard_map/ppermute | solution.py:25
  310.6 26.7 %collective-permute-start.9 = (f32[20,16,3]{2,0,1:T(8,128)}, f32[20,16,3]{2,0,1:T(8,128)}, u32[]{:S(2)}, u32[]{:S(2)}) collective-permute-start(f32[20,16,3]{2,0,1:T(8,128)} %get-tuple-element.357), channel_id=1, source_target_pairs={{8,0},{16,8},{24,16},{9,1},{17,9},{25,17},{10,2},{18,10},{26,18},{... | collective-permute-start | bytes 11528 | tf_op jit(solution)/shard_map/ppermute | solution.py:26
  311.9 59.6 %collective-permute-start.4 = (f32[20,32,3]{2,1,0:T(8,128)}, f32[20,32,3]{2,1,0:T(8,128)S(1)}, u32[]{:S(2)}, u32[]{:S(2)}) collective-permute-start(f32[20,32,3]{2,1,0:T(8,128)} %get-tuple-element.352), channel_id=1, source_target_pairs={{0,8},{8,16},{16,24},{1,9},{9,17},{17,25},{2,10},{10,18},{18,26},{... | collective-permute-start | bytes 23048 | tf_op jit(solution)/shard_map/ppermute | solution.py:25
  318.5 54.3 %collective-permute-start.5 = (f32[20,32,3]{2,1,0:T(8,128)}, f32[20,32,3]{2,1,0:T(8,128)S(1)}, u32[]{:S(2)}, u32[]{:S(2)}) collective-permute-start(f32[20,32,3]{2,1,0:T(8,128)} %get-tuple-element.353), channel_id=1, source_target_pairs={{8,0},{16,8},{24,16},{9,1},{17,9},{25,17},{10,2},{18,10},{26,18},{... | collective-permute-start | bytes 23048 | tf_op jit(solution)/shard_map/ppermute | solution.py:26
  320.5 131.3 %collective-permute-start = (f32[3,32,32,1]{2,1,3,0:T(8,128)}, f32[3,32,32,1]{2,1,3,0:T(8,128)}, u32[]{:S(2)}, u32[]{:S(2)}) collective-permute-start(f32[3,32,32,1]{2,1,3,0:T(8,128)} %copy.1491), channel_id=1, source_target_pairs={{0,8},{8,16},{16,24},{1,9},{9,17},{17,25},{2,10},{10,18},{18,26},{... | collective-permute-start | bytes 36872 | tf_op jit(solution)/shard_map/ppermute | solution.py:25
  335.8 19.3 %collective-permute-start.18 = (f32[20,3,22]{0,2,1:T(8,128)}, f32[20,3,22]{0,2,1:T(8,128)S(1)}, u32[]{:S(2)}, u32[]{:S(2)}) collective-permute-start(f32[20,3,22]{0,2,1:T(8,128)} %get-tuple-element.362), channel_id=1, source_target_pairs={{0,2},{2,4},{4,6},{1,3},{3,5},{5,7},{8,10},{10,12},{12,14},{9,11},... | collective-permute-start | bytes 15848 | tf_op jit(solution)/shard_map/ppermute | solution.py:25
  337.3 19.1 %collective-permute-start.19 = (f32[20,3,22]{0,2,1:T(8,128)}, f32[20,3,22]{0,2,1:T(8,128)}, u32[]{:S(2)}, u32[]{:S(2)}) collective-permute-start(f32[20,3,22]{0,2,1:T(8,128)} %get-tuple-element.363), channel_id=1, source_target_pairs={{2,0},{4,2},{6,4},{3,1},{5,3},{7,5},{10,8},{12,10},{14,12},{11,9},... | collective-permute-start | bytes 15848 | tf_op jit(solution)/shard_map/ppermute | solution.py:26
  355.1 99.4 %collective-permute-start.1 = (f32[3,32,32,1]{2,1,3,0:T(8,128)}, f32[3,32,32,1]{2,1,3,0:T(8,128)}, u32[]{:S(2)}, u32[]{:S(2)}) collective-permute-start(f32[3,32,32,1]{2,1,3,0:T(8,128)} %copy.1492), channel_id=1, source_target_pairs={{8,0},{16,8},{24,16},{9,1},{17,9},{25,17},{10,2},{18,10},{26,18},{... | collective-permute-start | bytes 36872 | tf_op jit(solution)/shard_map/ppermute | solution.py:26
  356.4 43.5 %collective-permute-start.14 = (f32[20,3,38]{2,0,1:T(8,128)}, f32[20,3,38]{2,0,1:T(8,128)}, u32[]{:S(2)}, u32[]{:S(2)}) collective-permute-start(f32[20,3,38]{2,0,1:T(8,128)} %get-tuple-element.358), channel_id=1, source_target_pairs={{0,2},{2,4},{4,6},{1,3},{3,5},{5,7},{8,10},{10,12},{12,14},{9,11},... | collective-permute-start | bytes 27368 | tf_op jit(solution)/shard_map/ppermute | solution.py:25
  371.5 29.7 %collective-permute-start.15 = (f32[20,3,38]{2,0,1:T(8,128)}, f32[20,3,38]{2,0,1:T(8,128)S(1)}, u32[]{:S(2)}, u32[]{:S(2)}) collective-permute-start(f32[20,3,38]{2,0,1:T(8,128)} %get-tuple-element.359), channel_id=1, source_target_pairs={{2,0},{4,2},{6,4},{3,1},{5,3},{7,5},{10,8},{12,10},{14,12},{11,9},... | collective-permute-start | bytes 27368 | tf_op jit(solution)/shard_map/ppermute | solution.py:26
  373.5 92.0 %collective-permute-start.10 = (f32[20,3,70]{2,0,1:T(8,128)}, f32[20,3,70]{2,0,1:T(8,128)}, u32[]{:S(2)}, u32[]{:S(2)}) collective-permute-start(f32[20,3,70]{2,0,1:T(8,128)} %get-tuple-element.354), channel_id=1, source_target_pairs={{0,2},{2,4},{4,6},{1,3},{3,5},{5,7},{8,10},{10,12},{12,14},{9,11},... | collective-permute-start | bytes 50408 | tf_op jit(solution)/shard_map/ppermute | solution.py:25
  399.9 66.9 %collective-permute-start.11 = (f32[20,3,70]{2,0,1:T(8,128)}, f32[20,3,70]{2,0,1:T(8,128)}, u32[]{:S(2)}, u32[]{:S(2)}) collective-permute-start(f32[20,3,70]{2,0,1:T(8,128)} %get-tuple-element.355), channel_id=1, source_target_pairs={{2,0},{4,2},{6,4},{3,1},{5,3},{7,5},{10,8},{12,10},{14,12},{11,9},... | collective-permute-start | bytes 50408 | tf_op jit(solution)/shard_map/ppermute | solution.py:26
  401.2 203.9 %collective-permute-start.6 = (f32[20,3,134]{2,1,0:T(4,128)}, f32[20,3,134]{2,1,0:T(4,128)}, u32[]{:S(2)}, u32[]{:S(2)}) collective-permute-start(f32[20,3,134]{2,1,0:T(4,128)} %get-tuple-element.348), channel_id=1, source_target_pairs={{0,2},{2,4},{4,6},{1,3},{3,5},{5,7},{8,10},{10,12},{12,14},{9,11},... | collective-permute-start | bytes 96488 | tf_op jit(solution)/shard_map/ppermute | solution.py:25
  451.8 153.3 %collective-permute-start.7 = (f32[20,3,134]{2,1,0:T(4,128)}, f32[20,3,134]{2,1,0:T(4,128)}, u32[]{:S(2)}, u32[]{:S(2)}) collective-permute-start(f32[20,3,134]{2,1,0:T(4,128)} %get-tuple-element.349), channel_id=1, source_target_pairs={{2,0},{4,2},{6,4},{3,1},{5,3},{7,5},{10,8},{12,10},{14,12},{11,9},... | collective-permute-start | bytes 96488 | tf_op jit(solution)/shard_map/ppermute | solution.py:26
  459.7 377.6 %collective-permute-start.2 = (f32[3,32,1,130]{3,1,2,0:T(8,128)}, f32[3,32,1,130]{3,1,2,0:T(8,128)}, u32[]{:S(2)}, u32[]{:S(2)}) collective-permute-start(f32[3,32,1,130]{3,1,2,0:T(8,128)} %copy.1495), channel_id=1, source_target_pairs={{0,2},{2,4},{4,6},{1,3},{3,5},{5,7},{8,10},{10,12},{12,14},{9,11},... | collective-permute-start | bytes 149768 | tf_op jit(solution)/shard_map/ppermute | solution.py:25
  465.5 372.8 %collective-permute-start.3 = (f32[3,32,1,130]{3,1,2,0:T(8,128)}, f32[3,32,1,130]{3,1,2,0:T(8,128)}, u32[]{:S(2)}, u32[]{:S(2)}) collective-permute-start(f32[3,32,1,130]{3,1,2,0:T(8,128)} %copy.1496), channel_id=1, source_target_pairs={{2,0},{4,2},{6,4},{3,1},{5,3},{7,5},{10,8},{12,10},{14,12},{11,9},... | collective-permute-start | bytes 149768 | tf_op jit(solution)/shard_map/ppermute | solution.py:26
  (104 other events, 1475.3 us)
Sparse Core Ops, SparseCore 0:
  139.7 8.3 all-gather.2
where the time goes:
time: 976 us; the launch traced here: 962 us
  local copies, waits for them, and re-layouts  669 us (69%)
  other arithmetic  83.4 us (9%)
  starting transfers between devices  67.1 us (7%)
  matrix products  54.3 us (6%)
  blocking collectives  40.2 us (4%)
  loops' own time  24.6 us (3%)
  between operations  17.2 us (2%)
    slice x265, local copies, waits for them, and re-layouts, grouped_far(): padded[:, first_y:first_y + cells_y:2, first_x:first_x + cells_x:2]  295 us
    unnamed x257, local copies, waits for them, and re-layouts  80.5 us
    concatenate x28, local copies, waits for them, and re-layouts, grouped_far(): jnp.concatenate(pieces, axis=0)  64.8 us
    ppermute x10, starting transfers between devices, with_halo(): before = lax.ppermute(last, axis, up)  42.9 us
    dot_general x56, matrix products, apply_matrix(): jnp.einsum('ij,jyx->iyx', jnp.asarray(matrix, dtype=jnp.float32), level_f...  42 us
    all_gather x1, blocking collectives, local(): lax.all_gather(coarse_own[None], ('cell', 'level'), axis=0, tiled=True)  40.2 us
    reduce_sum x8, other arithmetic, near_band(): real_sum = real_sum + jnp.sum(weight * gap_x, axis=1)  36.7 us
    slice x1, local copies, waits for them, and re-layouts, local(): far_real, far_imag = evaluate(local_field, particles[0], particles[1])  35.7 us
  transfers between devices with their start and end apart: 23, of which 1 were waited for; matrix products, arithmetic and copies ran while one was open for 59% of the time, Pallas kernels for 0%

commit v1 on v0

--- a/solution.py
+++ b/solution.py
@@ -4,6 +4,8 @@
 import jax.numpy as jnp
 import numpy as np
 from jax import lax
+from jax.experimental import pallas as pl
+from jax.experimental.pallas import tpu as pltpu
 from jax.sharding import PartitionSpec as P
 
 ORDER = 10
@@ -154,15 +156,66 @@
     return jnp.stack(real_rows + imag_rows)
 
 
-def evaluate(local_field, pos_x, pos_y):
-    real_acc = jnp.broadcast_to(local_field[ORDER - 1], pos_x.shape)
-    imag_acc = jnp.broadcast_to(local_field[2 * ORDER - 1], pos_x.shape)
-    for l in range(ORDER - 2, -1, -1):
-        real_acc, imag_acc = (
-            real_acc * pos_x - imag_acc * pos_y + local_field[l],
-            real_acc * pos_y + imag_acc * pos_x + local_field[ORDER + l],
-        )
-    return (real_acc, imag_acc)
+BAND = 8
+GROUP = 8
+
+
+def near_kernel(src_ref, own_ref, local_ref, out_ref):
+    half_slots, cells_y, cells_x = own_ref.shape[1:]
+    slot_count = src_ref.shape[2]
+    scale = 1.0 / (2.0 * math.pi)
+
+    def one_block(index, carry):
+        row = pl.multiple_of((index // (half_slots // GROUP)) * BAND, BAND)
+        slot = (index % (half_slots // GROUP)) * GROUP
+        here = pl.ds(row, BAND)
+        target_x = [own_ref[0, slot + t, here, :] for t in range(GROUP)]
+        target_y = [own_ref[1, slot + t, here, :] for t in range(GROUP)]
+
+        def one_source(s, sums):
+            sums = list(sums)
+            for step_y in (-1, 0, 1):
+                there = pl.ds(row + 1 + step_y, BAND)
+                for step_x in (-1, 0, 1):
+                    source_x = src_ref[step_x + 1, 0, s, there, :] + float(step_x)
+                    source_y = src_ref[step_x + 1, 1, s, there, :] + float(step_y)
+                    strength = src_ref[step_x + 1, 2, s, there, :]
+                    for t in range(GROUP):
+                        gap_x = target_x[t] - source_x
+                        gap_y = target_y[t] - source_y
+                        square = gap_x * gap_x + (gap_y * gap_y + blob_square)
+                        weight = strength * pl.reciprocal(square, approx=True)
+                        sums[t] = sums[t] + weight * gap_x
+                        sums[GROUP + t] = sums[GROUP + t] + weight * gap_y
+            return tuple(sums)
+
+        zero = jnp.zeros((BAND, cells_x), jnp.float32)
+        sums = lax.fori_loop(0, slot_count, one_source, (zero,) * (2 * GROUP))
+        for t in range(GROUP):
+            real_acc = local_ref[ORDER - 1, here, :]
+            imag_acc = local_ref[2 * ORDER - 1, here, :]
+            for l in range(ORDER - 2, -1, -1):
+                real_acc, imag_acc = (
+                    real_acc * target_x[t] - imag_acc * target_y[t] + local_ref[l, here, :],
+                    real_acc * target_y[t] + imag_acc * target_x[t] + local_ref[ORDER + l, here, :],
+                )
+            out_ref[0, slot + t, here, :] = (imag_acc - sums[GROUP + t]) * scale
+            out_ref[1, slot + t, here, :] = (real_acc + sums[t]) * scale
+        return carry
+
+    lax.fori_loop(0, (cells_y // BAND) * (half_slots // GROUP), one_block, 0)
+
+
+def near_and_far(shifted, own, local_field):
+    vmem = pl.BlockSpec(memory_space=pltpu.VMEM)
+    return pl.pallas_call(
+        near_kernel,
+        out_shape=jax.ShapeDtypeStruct((2,) + own.shape[1:], jnp.float32),
+        in_specs=[vmem] * 3,
+        out_specs=vmem,
+        compiler_params=pltpu.CompilerParams(vmem_limit_bytes=48 * 1024 * 1024),
+        name="near_and_far",
+    )(shifted, own, local_field)
 
 
 def framing(level_field):
@@ -233,38 +286,8 @@
         local_field = grouped_far(
             framed_levels[k], 3, level_field.shape[1], level_field.shape[2]
         ) + downward(local_field)
-    far_real, far_imag = evaluate(local_field, particles[0], particles[1])
-    slot_count = framed.shape[1]
-    slot_base = lax.axis_index("rep") * half_slots
-    target_slots = slot_base + jnp.arange(half_slots, dtype=jnp.int32)
-    keep_mask = (target_slots[:, None] != jnp.arange(slot_count, dtype=jnp.int32)[None, :]).astype(
-        jnp.float32
-    )[:, :, None, None]
-    band_rows = 8
-
-    def near_band(row_start):
-        target = lax.dynamic_slice_in_dim(particles, row_start, band_rows, 2)
-        real_sum = jnp.zeros((half_slots, band_rows, cells_x), jnp.float32)
-        imag_sum = jnp.zeros((half_slots, band_rows, cells_x), jnp.float32)
-        for step_y in (-1, 0, 1):
-            row_band = lax.dynamic_slice_in_dim(framed, row_start + 1 + step_y, band_rows, 2)
-            for step_x in (-1, 0, 1):
-                source = row_band[:, :, :, 1 + step_x : 1 + step_x + cells_x]
-                gap_x = target[0][:, None] - source[0][None] - step_x
-                gap_y = target[1][:, None] - source[1][None] - step_y
-                weight = source[2][None] / (gap_x * gap_x + gap_y * gap_y + blob_square)
-                if step_x == 0 and step_y == 0:
-                    weight = weight * keep_mask
-                real_sum = real_sum + jnp.sum(weight * gap_x, axis=1)
-                imag_sum = imag_sum - jnp.sum(weight * gap_y, axis=1)
-        return jnp.stack([real_sum, imag_sum])
-
-    starts = jnp.arange(0, cells_y, band_rows, dtype=jnp.int32)
-    bands = lax.map(near_band, starts)
-    near = bands.transpose(1, 2, 0, 3, 4).reshape(2, half_slots, cells_y, cells_x)
-    real_part = near[0] + far_real
-    imag_part = near[1] + far_imag
-    return jnp.stack([imag_part, real_part]) / (2.0 * math.pi)
+    shifted = jnp.stack([framed[:, :, :, d : d + cells_x] for d in range(3)])
+    return near_and_far(shifted, particles, local_field)
 
 
 def solution(mesh):

time: 976 us -> 853 us (0.87)
  local copies, waits for them, and re-layouts: 669 us -> 566 us
  other arithmetic: 83.4 us -> 39.5 us
  Pallas kernels: 0 us -> 37.9 us
  loops' own time: 24.6 us -> 0 us
    slice x25 -> x1, local copies, waits for them, and re-layouts: 48.6 us -> 0.22 us  [the longest x1 35.7 us: local(): far_real, far_imag = evaluate(local_field, particles[0], particles[1])]
    pallas_call x0 -> x1, Pallas kernels: none -> 37.9 us  [near_and_far(): pl.pallas_call(near_kernel, out_shape=jax.ShapeDtypeStruct((2,) + own.sha...]
    reduce_sum x8 -> x0, other arithmetic: 36.7 us -> none  [near_band(): real_sum = real_sum + jnp.sum(weight * gap_x, axis=1)]
    div x4 -> x0, local copies, waits for them, and re-layouts: 29 us -> none  [near_band(): weight = source[2][None] / (gap_x * gap_x + gap_y * gap_y + blob_square)]
    another operation x1 -> x0, loops' own time: 24.6 us -> none  [local(): bands = lax.map(near_band, starts)]
    add x18 -> x0, local copies, waits for them, and re-layouts: 19.9 us -> none  [the longest x9 10.3 us: evaluate(): real_acc * pos_x - imag_acc * pos_y + local_field[l]]
    unnamed x257 -> x199, local copies, waits for them, and re-layouts: 80.5 us -> 85.6 us
  transfers between devices with their start and end apart: 23 -> 23, of which waited for: 1 -> 2; matrix products, arithmetic and copies ran while one was open for 59% -> 60% of each run, Pallas kernels for 0% -> 0%
where the time goes in v1:
time: 853 us; the launch traced here: 839 us
  local copies, waits for them, and re-layouts  566 us (66%)
  starting transfers between devices  67.7 us (8%)
  matrix products  54.3 us (6%)
  blocking collectives  43.1 us (5%)
  other arithmetic  39.5 us (5%)
  Pallas kernels  37.9 us (4%)
  between operations  16.8 us (2%)
  waiting for transfers between devices  14.3 us (2%)
    slice x265, local copies, waits for them, and re-layouts, grouped_far(): padded[:, first_y:first_y + cells_y:2, first_x:first_x + cells_x:2]  293 us
    unnamed x199, local copies, waits for them, and re-layouts  85.6 us
    concatenate x28, local copies, waits for them, and re-layouts, grouped_far(): jnp.concatenate(pieces, axis=0)  64.7 us
    ppermute x10, starting transfers between devices, with_halo(): before = lax.ppermute(last, axis, up)  43.2 us
    all_gather x1, blocking collectives, local(): lax.all_gather(coarse_own[None], ('cell', 'level'), axis=0, tiled=True)  43.1 us
    dot_general x56, matrix products, apply_matrix(): jnp.einsum('ij,jyx->iyx', jnp.asarray(matrix, dtype=jnp.float32), level_f...  42 us
    pallas_call x1, Pallas kernels, near_and_far(): pl.pallas_call(near_kernel, out_shape=jax.ShapeDtypeStruct((2,) + own.sha...  37.9 us
    scatter x1, local copies, waits for them, and re-layouts, local(): resident.at[:, arrived_at.reshape(-1)]  32.7 us
  transfers between devices with their start and end apart: 23, of which 2 were waited for; matrix products, arithmetic and copies ran while one was open for 60% of the time, Pallas kernels for 0%

profile of v1, /device:TPU:0, one launch (start us, length us, event | category | flops | bytes accessed | tf_op | source)
XLA Modules:
  0.0 839.2 jit_solution(2604201518847392055)
XLA Ops:
  12.9 16.1 %scatter_custom_fusion.1 = s32[4096]{0:T(1024)} fusion(s32[4096]{0:T(1024)S(1)} %broadcast_select_fusion.1, s32[4096]{0:T(1024)S(1)} %bitcast.821, s32[]{:T(128)} %constant.28.clone.1), kind=kCustom, calls=%fused_computation.252 | custom fusion | bytes 16388
  29.0 6.3 all-to-all-start
  41.7 12.3 %scatter_custom_fusion.2 = f32[3,4096]{0,1:T(8,128)} fusion(s32[4096]{0:T(1024)S(1)} %broadcast_select_fusion, f32[4096,3]{1,0:T(8,128)} %copy.474, f32[]{:T(128)} %constant.34.clone.1), kind=kCustom, calls=%fused_computation.80 | custom fusion | bytes 49664
  56.8 16.0 %copy.476 = f32[3,65536]{0,1:T(8,128)} copy(f32[3,65536]{1,0:T(4,128)S(1)} %pad_maximum_fusion.2) | data formatting | bytes 1572864 | tf_op jit(solution)/shard_map/concatenate | solution.py:250
  72.8 5.1 all-to-all-start.1
  77.9 5.7 all-to-all-done.1
  85.6 32.7 %scatter_fusion = f32[3,65536]{0,1:T(8,128)} fusion(f32[3,65536]{0,1:T(8,128)} %copy.476, s32[4096]{0:T(1024)S(1)} %bitcast.816, f32[4096,3]{1,0:T(8,128)} %copy.477), kind=kCustom, calls=%fused_computation | custom fusion | bytes 163840 | tf_op jit(solution)/shard_map/scatter | solution.py:251
  118.2 20.2 %copy.775.own_ref = f32[3,16,32,128]{3,2,1,0:T(8,128)} copy(f32[3,16,32,128]{0,3,2,1:T(8,128)} %bitcast.752) | data formatting | bytes 1572864 | tf_op jit(solution)/shard_map/reshape | solution.py:252
  138.5 8.5 %all-gather.3.cloned.1.call-done = f32[3,32,32,128]{3,2,1,0:T(8,128)} async-done(((f32[3,16,32,128]{3,2,1,0:T(8,128)}), f32[3,32,32,128]{3,2,1,0:T(8,128)}) %all-gather.3.cloned.1.call-update) | async-done | bytes 1572880 | tf_op jit(solution)/shard_map/all_gather | solution.py:253
  176.9 43.1 %all-gather = f32[320,2,8]{2,1,0:T(2,128)S(1)} all-gather(f32[20,2,8]{2,1,0:T(2,128)S(1)} %copy.739), channel_id=2, replica_groups=mesh['cell'=4,'level'=4,'rep'=2] {'cell','level'}, dimensions={0}, use_global_device_ids=true | all-gather | bytes 21760 | tf_op jit(solution)/shard_map/all_gather | solution.py:263
  265.1 4.6 collective-permute-start.12
  271.0 5.2 collective-permute-start.8
  286.3 4.6 collective-permute-start.4
  294.8 5.2 collective-permute-start
  330.4 5.3 collective-permute-start.14
  347.7 5.2 collective-permute-start.10
  375.4 5.4 collective-permute-start.6
  433.9 5.2 collective-permute-start.2
  723.6 9.6 %concatenate.134 = f32[540,16,64]{0,2,1:T(8,128)} concatenate(f32[20,16,64]{0,2,1:T(8,128)S(1)} %copy.777, f32[20,16,64]{0,2,1:T(8,128)} %copy.778, f32[20,16,64]{0,2,1:T(8,128)} %copy.779, f32[20,16,64]{0,2,1:T(8,128)} %copy.780, f32[20,16,64]{0,2,1:T(8,128)} %copy.781, f32[20,16,64]{0,2,1:T(8,128)} %copy.782, f32[20,16,64]{0,2,1:T(8,128)} %copy.783, f32[20,16,64]{0,2,1:T(8,128)} %copy.784, ...), dimensions={0} | concatenate | bytes 4423680 | tf_op jit(solution)/shard_map/concatenate | solution.py:118
  733.2 9.6 %concatenate.135 = f32[540,16,64]{0,2,1:T(8,128)} concatenate(f32[20,16,64]{0,2,1:T(8,128)S(1)} %copy.777, f32[20,16,64]{0,2,1:T(8,128)} %copy.778, f32[20,16,64]{0,2,1:T(8,128)} %copy.779, f32[20,16,64]{0,2,1:T(8,128)} %copy.780, f32[20,16,64]{0,2,1:T(8,128)} %copy.781, f32[20,16,64]{0,2,1:T(8,128)} %copy.782, f32[20,16,64]{0,2,1:T(8,128)} %copy.783, f32[20,16,64]{0,2,1:T(8,128)} %copy.804, ...), dimensions={0} | concatenate | bytes 4423680 | tf_op jit(solution)/shard_map/concatenate | solution.py:118
  742.8 9.7 %concatenate.136 = f32[540,16,64]{0,2,1:T(8,128)} concatenate(f32[20,16,64]{0,2,1:T(8,128)S(1)} %copy.777, f32[20,16,64]{0,2,1:T(8,128)} %copy.778, f32[20,16,64]{0,2,1:T(8,128)} %copy.779, f32[20,16,64]{0,2,1:T(8,128)} %copy.780, f32[20,16,64]{0,2,1:T(8,128)} %copy.781, f32[20,16,64]{0,2,1:T(8,128)} %copy.782, f32[20,16,64]{0,2,1:T(8,128)} %copy.783, f32[20,16,64]{0,2,1:T(8,128)} %copy.804, ...), dimensions={0} | concatenate | bytes 4423680 | tf_op jit(solution)/shard_map/concatenate | solution.py:118
  752.5 9.6 %concatenate.137 = f32[540,16,64]{0,2,1:T(8,128)} concatenate(f32[20,16,64]{0,2,1:T(8,128)S(1)} %copy.777, f32[20,16,64]{0,2,1:T(8,128)} %copy.778, f32[20,16,64]{0,2,1:T(8,128)} %copy.779, f32[20,16,64]{0,2,1:T(8,128)} %copy.780, f32[20,16,64]{0,2,1:T(8,128)} %copy.781, f32[20,16,64]{0,2,1:T(8,128)} %copy.782, f32[20,16,64]{0,2,1:T(8,128)} %copy.783, f32[20,16,64]{0,2,1:T(8,128)} %copy.804, ...), dimensions={0} | concatenate | bytes 4423680 | tf_op jit(solution)/shard_map/concatenate | solution.py:118
  762.2 5.7 convolution_bitcast_fusion.7
  794.2 37.9 %near_and_far.1 = f32[2,16,32,128]{3,2,1,0:T(8,128)} custom-call(f32[3,3,32,34,128]{4,3,2,1,0:T(8,128)} %pad_maximum_fusion.src_ref, f32[3,16,32,128]{3,2,1,0:T(8,128)S(1)} %copy-done, f32[20,32,128]{2,1,0:T(8,128)S(1)} %copy.762.local_ref), custom_call_target="tpu_custom_call" | custom-call | tf_op jit(solution)/shard_map/near_and_far/pallas_call | solution.py:211
  (735 shorter events, 533.9 us)
Async XLA Ops:
  29.0 43.8 %all-to-all-start = ((s32[1,4,1024]{2,0,1:T(1,128)}), s32[1,4,1024]{2,0,1:T(1,128)S(1)}, u32[]{:S(2)}, u32[]{:S(2)}) async-start(s32[1,4,1024]{2,0,1:T(1,128)} %bitcast.8), calls=%async_computation | async-start | bytes 32768 | tf_op jit(solution)/shard_map/all_to_all | solution.py:248
  72.8 10.8 %all-to-all-start.1 = ((f32[3,4,1024]{2,0,1:T(4,128)}), f32[3,4,1024]{2,0,1:T(4,128)S(1)}, u32[]{:S(2)}, u32[]{:S(2)}) async-start(f32[3,4,1024]{2,0,1:T(4,128)} %copy.475), calls=%async_computation.1 | async-start | bytes 131072 | tf_op jit(solution)/shard_map/all_to_all | solution.py:247
  77.9 69.1 %all-gather.3.cloned.1.call-start = ((), (), s32[]{:S(2)}) async-start(), calls=%async_computation.2 | async-start | bytes 2359296 | tf_op jit(solution)/shard_map/all_gather | solution.py:253
  165.1 147.9 %copy-start.9 = (f32[20,16,64]{2,0,1:T(8,128)}, f32[20,16,64]{2,0,1:T(8,128)S(1)}, u32[]{:S(2)}) copy-start(f32[20,16,64]{2,0,1:T(8,128)S(1)} %fusion) | copy-start | bytes 245764
  262.6 22.4 %collective-permute-start.16 = (f32[20,4,3]{0,2,1:T(4,128)S(1)}, f32[20,4,3]{0,2,1:T(4,128)S(1)}, u32[]{:S(2)}, u32[]{:S(2)}) collective-permute-start(f32[20,4,3]{0,2,1:T(4,128)S(1)} %get-tuple-element.54), channel_id=1, source_target_pairs={{0,8},{8,16},{16,24},{1,9},{9,17},{17,25},{2,10},{10,18},{18,26},{... | collective-permute-start | bytes 2888 | tf_op jit(solution)/shard_map/ppermute | solution.py:27
  263.8 22.4 %collective-permute-start.17 = (f32[20,4,3]{0,2,1:T(4,128)S(1)}, f32[20,4,3]{0,2,1:T(4,128)S(1)}, u32[]{:S(2)}, u32[]{:S(2)}) collective-permute-start(f32[20,4,3]{0,2,1:T(4,128)S(1)} %get-tuple-element.55), channel_id=1, source_target_pairs={{8,0},{16,8},{24,16},{9,1},{17,9},{25,17},{10,2},{18,10},{26,18},{... | collective-permute-start | bytes 2888 | tf_op jit(solution)/shard_map/ppermute | solution.py:28
  265.1 27.8 %collective-permute-start.12 = (f32[20,8,3]{2,0,1:T(8,128)S(1)}, f32[20,8,3]{2,0,1:T(8,128)S(1)}, u32[]{:S(2)}, u32[]{:S(2)}) collective-permute-start(f32[20,8,3]{2,0,1:T(8,128)S(1)} %get-tuple-element.50), channel_id=1, source_target_pairs={{0,8},{8,16},{16,24},{1,9},{9,17},{17,25},{2,10},{10,18},{18,26},{... | collective-permute-start | bytes 5768 | tf_op jit(solution)/shard_map/ppermute | solution.py:27
  269.7 24.5 %collective-permute-start.13 = (f32[20,8,3]{2,0,1:T(8,128)}, f32[20,8,3]{2,0,1:T(8,128)S(1)}, u32[]{:S(2)}, u32[]{:S(2)}) collective-permute-start(f32[20,8,3]{2,0,1:T(8,128)} %get-tuple-element.51), channel_id=1, source_target_pairs={{8,0},{16,8},{24,16},{9,1},{17,9},{25,17},{10,2},{18,10},{26,18},{... | collective-permute-start | bytes 5768 | tf_op jit(solution)/shard_map/ppermute | solution.py:28
  271.0 39.3 %collective-permute-start.8 = (f32[20,16,3]{2,0,1:T(8,128)}, f32[20,16,3]{2,0,1:T(8,128)}, u32[]{:S(2)}, u32[]{:S(2)}) collective-permute-start(f32[20,16,3]{2,0,1:T(8,128)} %get-tuple-element.46), channel_id=1, source_target_pairs={{0,8},{8,16},{16,24},{1,9},{9,17},{17,25},{2,10},{10,18},{18,26},{... | collective-permute-start | bytes 11528 | tf_op jit(solution)/shard_map/ppermute | solution.py:27
  285.0 26.7 %collective-permute-start.9 = (f32[20,16,3]{2,0,1:T(8,128)}, f32[20,16,3]{2,0,1:T(8,128)}, u32[]{:S(2)}, u32[]{:S(2)}) collective-permute-start(f32[20,16,3]{2,0,1:T(8,128)} %get-tuple-element.47), channel_id=1, source_target_pairs={{8,0},{16,8},{24,16},{9,1},{17,9},{25,17},{10,2},{18,10},{26,18},{... | collective-permute-start | bytes 11528 | tf_op jit(solution)/shard_map/ppermute | solution.py:28
  286.3 59.4 %collective-permute-start.4 = (f32[20,32,3]{2,1,0:T(8,128)}, f32[20,32,3]{2,1,0:T(8,128)S(1)}, u32[]{:S(2)}, u32[]{:S(2)}) collective-permute-start(f32[20,32,3]{2,1,0:T(8,128)} %get-tuple-element.42), channel_id=1, source_target_pairs={{0,8},{8,16},{16,24},{1,9},{9,17},{17,25},{2,10},{10,18},{18,26},{... | collective-permute-start | bytes 23048 | tf_op jit(solution)/shard_map/ppermute | solution.py:27
  292.9 54.1 %collective-permute-start.5 = (f32[20,32,3]{2,1,0:T(8,128)}, f32[20,32,3]{2,1,0:T(8,128)S(1)}, u32[]{:S(2)}, u32[]{:S(2)}) collective-permute-start(f32[20,32,3]{2,1,0:T(8,128)} %get-tuple-element.43), channel_id=1, source_target_pairs={{8,0},{16,8},{24,16},{9,1},{17,9},{25,17},{10,2},{18,10},{26,18},{... | collective-permute-start | bytes 23048 | tf_op jit(solution)/shard_map/ppermute | solution.py:28
  294.8 131.1 %collective-permute-start = (f32[3,32,32,1]{2,1,3,0:T(8,128)}, f32[3,32,32,1]{2,1,3,0:T(8,128)}, u32[]{:S(2)}, u32[]{:S(2)}) collective-permute-start(f32[3,32,32,1]{2,1,3,0:T(8,128)} %copy.479), channel_id=1, source_target_pairs={{0,8},{8,16},{16,24},{1,9},{9,17},{17,25},{2,10},{10,18},{18,26},{... | collective-permute-start | bytes 36872 | tf_op jit(solution)/shard_map/ppermute | solution.py:27
  310.3 18.9 %collective-permute-start.18 = (f32[20,3,22]{0,2,1:T(8,128)}, f32[20,3,22]{0,2,1:T(8,128)S(1)}, u32[]{:S(2)}, u32[]{:S(2)}) collective-permute-start(f32[20,3,22]{0,2,1:T(8,128)} %get-tuple-element.52), channel_id=1, source_target_pairs={{0,2},{2,4},{4,6},{1,3},{3,5},{5,7},{8,10},{10,12},{12,14},{9,11},... | collective-permute-start | bytes 15848 | tf_op jit(solution)/shard_map/ppermute | solution.py:27
  311.7 18.7 %collective-permute-start.19 = (f32[20,3,22]{0,2,1:T(8,128)}, f32[20,3,22]{0,2,1:T(8,128)}, u32[]{:S(2)}, u32[]{:S(2)}) collective-permute-start(f32[20,3,22]{0,2,1:T(8,128)} %get-tuple-element.53), channel_id=1, source_target_pairs={{2,0},{4,2},{6,4},{3,1},{5,3},{7,5},{10,8},{12,10},{14,12},{11,9},... | collective-permute-start | bytes 15848 | tf_op jit(solution)/shard_map/ppermute | solution.py:28
  329.1 99.5 %collective-permute-start.1 = (f32[3,32,32,1]{2,1,3,0:T(8,128)}, f32[3,32,32,1]{2,1,3,0:T(8,128)}, u32[]{:S(2)}, u32[]{:S(2)}) collective-permute-start(f32[3,32,32,1]{2,1,3,0:T(8,128)} %copy.480), channel_id=1, source_target_pairs={{8,0},{16,8},{24,16},{9,1},{17,9},{25,17},{10,2},{18,10},{26,18},{... | collective-permute-start | bytes 36872 | tf_op jit(solution)/shard_map/ppermute | solution.py:28
  330.4 43.6 %collective-permute-start.14 = (f32[20,3,38]{2,0,1:T(8,128)}, f32[20,3,38]{2,0,1:T(8,128)}, u32[]{:S(2)}, u32[]{:S(2)}) collective-permute-start(f32[20,3,38]{2,0,1:T(8,128)} %get-tuple-element.48), channel_id=1, source_target_pairs={{0,2},{2,4},{4,6},{1,3},{3,5},{5,7},{8,10},{10,12},{12,14},{9,11},... | collective-permute-start | bytes 27368 | tf_op jit(solution)/shard_map/ppermute | solution.py:27
  345.7 29.6 %collective-permute-start.15 = (f32[20,3,38]{2,0,1:T(8,128)}, f32[20,3,38]{2,0,1:T(8,128)S(1)}, u32[]{:S(2)}, u32[]{:S(2)}) collective-permute-start(f32[20,3,38]{2,0,1:T(8,128)} %get-tuple-element.49), channel_id=1, source_target_pairs={{2,0},{4,2},{6,4},{3,1},{5,3},{7,5},{10,8},{12,10},{14,12},{11,9},... | collective-permute-start | bytes 27368 | tf_op jit(solution)/shard_map/ppermute | solution.py:28
  347.7 91.4 %collective-permute-start.10 = (f32[20,3,70]{2,0,1:T(8,128)}, f32[20,3,70]{2,0,1:T(8,128)}, u32[]{:S(2)}, u32[]{:S(2)}) collective-permute-start(f32[20,3,70]{2,0,1:T(8,128)} %get-tuple-element.44), channel_id=1, source_target_pairs={{0,2},{2,4},{4,6},{1,3},{3,5},{5,7},{8,10},{10,12},{12,14},{9,11},... | collective-permute-start | bytes 50408 | tf_op jit(solution)/shard_map/ppermute | solution.py:27
  374.1 66.6 %collective-permute-start.11 = (f32[20,3,70]{2,0,1:T(8,128)}, f32[20,3,70]{2,0,1:T(8,128)}, u32[]{:S(2)}, u32[]{:S(2)}) collective-permute-start(f32[20,3,70]{2,0,1:T(8,128)} %get-tuple-element.45), channel_id=1, source_target_pairs={{2,0},{4,2},{6,4},{3,1},{5,3},{7,5},{10,8},{12,10},{14,12},{11,9},... | collective-permute-start | bytes 50408 | tf_op jit(solution)/shard_map/ppermute | solution.py:28
  375.4 203.5 %collective-permute-start.6 = (f32[20,3,134]{2,1,0:T(4,128)}, f32[20,3,134]{2,1,0:T(4,128)}, u32[]{:S(2)}, u32[]{:S(2)}) collective-permute-start(f32[20,3,134]{2,1,0:T(4,128)} %get-tuple-element.40), channel_id=1, source_target_pairs={{0,2},{2,4},{4,6},{1,3},{3,5},{5,7},{8,10},{10,12},{12,14},{9,11},... | collective-permute-start | bytes 96488 | tf_op jit(solution)/shard_map/ppermute | solution.py:27
  426.0 152.9 %collective-permute-start.7 = (f32[20,3,134]{2,1,0:T(4,128)}, f32[20,3,134]{2,1,0:T(4,128)}, u32[]{:S(2)}, u32[]{:S(2)}) collective-permute-start(f32[20,3,134]{2,1,0:T(4,128)} %get-tuple-element.41), channel_id=1, source_target_pairs={{2,0},{4,2},{6,4},{3,1},{5,3},{7,5},{10,8},{12,10},{14,12},{11,9},... | collective-permute-start | bytes 96488 | tf_op jit(solution)/shard_map/ppermute | solution.py:28
  433.9 353.0 %collective-permute-start.2 = (f32[3,32,1,130]{3,2,1,0:T(1,128)}, f32[3,32,1,130]{3,2,1,0:T(1,128)}, u32[]{:S(2)}, u32[]{:S(2)}) collective-permute-start(f32[3,32,1,130]{3,2,1,0:T(1,128)} %get-tuple-element.26), channel_id=1, source_target_pairs={{0,2},{2,4},{4,6},{1,3},{3,5},{5,7},{8,10},{10,12},{12,14},{9,11},... | collective-permute-start | bytes 149768 | tf_op jit(solution)/shard_map/ppermute | solution.py:27
  439.1 347.8 %collective-permute-start.3 = (f32[3,32,1,130]{3,2,1,0:T(1,128)}, f32[3,32,1,130]{3,2,1,0:T(1,128)}, u32[]{:S(2)}, u32[]{:S(2)}) collective-permute-start(f32[3,32,1,130]{3,2,1,0:T(1,128)} %get-tuple-element.27), channel_id=1, source_target_pairs={{2,0},{4,2},{6,4},{3,1},{5,3},{7,5},{10,8},{12,10},{14,12},{11,9},... | collective-permute-start | bytes 149768 | tf_op jit(solution)/shard_map/ppermute | solution.py:28
  (71 other events, 1356.3 us)
Sparse Core Ops, SparseCore 0:
  138.6 8.3 all-gather.2

commit v2 on v1

v2 whole, which is shorter than its diff:
```python
import functools
import math

import jax
import jax.numpy as jnp
import numpy as np
from jax import lax
from jax.experimental import pallas as pl
from jax.experimental.pallas import tpu as pltpu
from jax.sharding import PartitionSpec as P

ORDER = 10
HALO_LEVELS = 4
CAP = 1024
BAND = 8
GROUP = 8
FRONT = 8


precise = lax.Precision.HIGHEST
blob_square = 0.09


def real_form(matrix):
    top_rows = np.concatenate([matrix.real, -matrix.imag], axis=1)
    low_rows = np.concatenate([matrix.imag, matrix.real], axis=1)
    return np.concatenate([top_rows, low_rows], axis=0)


def child_offset(parity_x, parity_y):
    return complex((parity_x - 0.5) / 2.0, (parity_y - 0.5) / 2.0)


def upward_table(parity_x, parity_y):
    offset = child_offset(parity_x, parity_y)
    matrix = np.zeros((ORDER, ORDER), complex)
    for k in range(ORDER):
        for m in range(k + 1):
            matrix[k, m] = math.comb(k, m) * 0.5**m * offset ** (k - m)
    return real_form(matrix)


def downward_table(parity_x, parity_y):
    offset = child_offset(parity_x, parity_y)
    matrix = np.zeros((ORDER, ORDER), complex)
    for m in range(ORDER):
        for l in range(m, ORDER):
            matrix[m, l] = 0.5 ** (m + 1) * math.comb(l, m) * offset ** (l - m)
    return real_form(matrix)


def far_table(step_x, step_y):
    distance = complex(step_x, step_y)
    matrix = np.zeros((ORDER, ORDER), complex)
    for l in range(ORDER):
        for k in range(ORDER):
            matrix[l, k] = (-1) ** (k + 1) * math.comb(k + l, l) * distance ** (-(k + l + 1))
    return real_form(matrix)


CHANNELS = 2 * ORDER
PITCH = 24
HIGH = dict(precision=lax.Precision.HIGHEST, preferred_element_type=jnp.float32)


def pack_starts(cells_y):
    starts = [0]
    for k in range(HALO_LEVELS):
        used = CHANNELS * (cells_y >> k)
        starts.append(starts[-1] + -(-used // 128) * 128)
    return starts


def upward_matrix():
    blocks = [upward_table(px, py) for px in (0, 1) for py in (0, 1)]
    matrix = np.zeros((PITCH, 4 * CHANNELS), np.float32)
    matrix[:CHANNELS] = np.concatenate(blocks, axis=1)
    return matrix


def level_matrix():
    matrix = np.zeros((4 * CHANNELS, 7 * 6 * CHANNELS + 2 * PITCH))
    for px in (0, 1):
        for py in (0, 1):
            rows = slice((2 * px + py) * CHANNELS, (2 * px + py + 1) * CHANNELS)
            for step_x in range(-2 - px, 4 - px):
                for step_y in range(-2 - py, 4 - py):
                    if max(abs(step_x), abs(step_y)) <= 1:
                        continue
                    first = ((step_x + 3) * 6 + step_y + py + 2) * CHANNELS
                    matrix[rows, first : first + CHANNELS] = far_table(step_x, step_y)
            first = 42 * CHANNELS + px * PITCH
            matrix[rows, first : first + CHANNELS] = downward_table(px, py)
    high = np.asarray(matrix, np.float32).astype(jnp.bfloat16)
    low = (matrix - high.astype(np.float64)).astype(np.float32).astype(jnp.bfloat16)
    return np.concatenate([high, low], axis=0)


def top_steps(cells):
    return [d for d in range(1 - cells, cells) if abs(d) >= 2]


def top_matrix(cells):
    steps = top_steps(cells)
    matrix = np.zeros((PITCH, PITCH * len(steps)), np.float32)
    for i, step in enumerate(steps):
        matrix[:CHANNELS, i * PITCH : i * PITCH + CHANNELS] = far_table(step, 0)
    return matrix


def lanes_of(shape):
    return lax.broadcasted_iota(jnp.int32, shape, len(shape) - 1)


def shifted_lanes(value, halo, distance):
    width = value.shape[-1]
    if distance == 0:
        return value
    lane = lanes_of(value.shape)
    if distance > 0:
        return pltpu.roll(jnp.where(lane < distance, halo, value), width - distance, value.ndim - 1)
    return pltpu.roll(jnp.where(lane >= width + distance, halo, value), -distance, value.ndim - 1)


def raise_level(matrix, level_value, cells_y, stride):
    wide = level_value.shape[-1]
    parts = []
    for row in range(cells_y // 2):
        here = level_value[2 * CHANNELS * row : 2 * CHANNELS * (row + 1)]
        parts.append(jnp.concatenate([here, pltpu.roll(here, wide - stride, 1)], axis=0))
    product = jnp.dot(matrix, jnp.concatenate(parts, axis=1), **HIGH)
    return [product[:CHANNELS, wide * row : wide * (row + 1)] for row in range(cells_y // 2)]


def upward_kernel(place_ref, own_ref, other_ref, up_ref, zero_ref, one_ref, two_ref, three_ref, four_ref, pack_ref):
    slots, cells_y, cells_x = own_ref.shape[1:]
    levels = [zero_ref, one_ref, two_ref, three_ref]
    for row in range(0, cells_y, BAND):
        here = pl.ds(row, BAND)

        def one_slot(s, sums):
            sums = list(sums)
            for parts_ref in (own_ref, other_ref):
                pos_x, pos_y = parts_ref[0, s, here, :], parts_ref[1, s, here, :]
                real, imag = parts_ref[2, s, here, :], jnp.zeros_like(pos_x)
                for k in range(ORDER):
                    sums[k] = sums[k] + real
                    sums[ORDER + k] = sums[ORDER + k] + imag
                    real, imag = real * pos_x - imag * pos_y, real * pos_y + imag * pos_x
            return tuple(sums)

        zero = jnp.zeros((BAND, cells_x), jnp.float32)
        sums = lax.fori_loop(0, slots, one_slot, (zero,) * CHANNELS)
        for c in range(CHANNELS):
            zero_ref[pl.ds(row * CHANNELS + c, BAND, stride=CHANNELS), :] = sums[c]
    up = up_ref[...]
    pack_ref[...] = jnp.zeros_like(pack_ref)
    starts = pack_starts(cells_y)
    for k in range(HALO_LEVELS):
        count = cells_y >> k
        value = levels[k][...]
        raised = raise_level(up, value, count, 1 << k)
        if k < HALO_LEVELS - 1:
            for row, piece in enumerate(raised):
                levels[k + 1][row * CHANNELS : (row + 1) * CHANNELS, :] = piece
        else:
            lane = lanes_of((cells_x, cells_x))
            source = lax.broadcasted_iota(jnp.int32, (cells_x, cells_x), 0)
            width = cells_x >> HALO_LEVELS
            wanted = (lane - place_ref[0] * width) * (1 << HALO_LEVELS)
            choose = ((source == wanted) & (wanted >= 0)).astype(jnp.float32)
            four = jnp.concatenate(raised, axis=0)
            four_ref[...] = jnp.dot(four, choose, **HIGH)
        which = lax.broadcasted_iota(jnp.int32, (8, cells_x), 0)
        pick = (lanes_of((8, cells_x)) == edge_lane(which, k, cells_x)).astype(jnp.float32)
        pack_ref[:, starts[k] : starts[k] + count * CHANNELS] = lax.dot_general(
            pick, value, (((1,), (1,)), ((), ())), **HIGH
        )


def edge_lane(which, k, cells_x):
    near = which * (1 << k)
    far = cells_x + (which - 4) * (1 << k)
    return jnp.where(which < 2, near, jnp.where(which < 4, far, -1))


def far_rows(matrix_ref, source_ref, halo_ref, count, stride, parent_ref, out_ref, stage_ref):
    wide = source_ref.shape[-1]
    rows = 6 * CHANNELS
    outer = count // 2
    chunk = min(outer, 4)

    def one_chunk(index, carry):
        for j in range(chunk):
            row = index * chunk + j
            begin = row * 2 * CHANNELS
            if not isinstance(begin, int):
                begin = pl.multiple_of(begin, 8)
            here = pl.ds(begin, rows)
            value = source_ref[here, :]
            halo = 0.0 if halo_ref is None else halo_ref[here, :]
            lanes = slice(j * wide, (j + 1) * wide)
            for step in range(-3, 4):
                first = (step + 3) * rows
                stage_ref[first : first + rows, lanes] = shifted_lanes(value, halo, step * stride)
            above = row * PITCH
            if not isinstance(above, int):
                above = pl.multiple_of(above, 8)
            parent = parent_ref[pl.ds(above, PITCH), :]
            stage_ref[7 * rows : 7 * rows + PITCH, lanes] = parent
            stage_ref[7 * rows + PITCH :, lanes] = pltpu.roll(parent, stride, 1)
        full = stage_ref[:, : chunk * wide]
        high = full.astype(jnp.bfloat16)
        low = (full - high.astype(jnp.float32)).astype(jnp.bfloat16)
        both = jnp.dot(matrix_ref[...], high, preferred_element_type=jnp.float32)
        rest = jnp.dot(matrix_ref[: 4 * CHANNELS, :], low, preferred_element_type=jnp.float32)
        total = both[: 4 * CHANNELS] + (both[4 * CHANNELS :] + rest)
        lane = lanes_of((2 * CHANNELS, wide))
        odd = lax.rem(lane // stride, 2) == 1
        for j in range(chunk):
            lanes = slice(j * wide, (j + 1) * wide)
            chosen = jnp.where(odd, total[2 * CHANNELS :, lanes], total[: 2 * CHANNELS, lanes])
            for py in (0, 1):
                begin = (2 * (index * chunk + j) + py) * PITCH
                if not isinstance(begin, int):
                    begin = pl.multiple_of(begin, 8)
                out_ref[pl.ds(begin, CHANNELS), :] = chosen[py * CHANNELS : (py + 1) * CHANNELS]
        return carry

    if outer == chunk:
        one_chunk(0, 0)
    else:
        lax.fori_loop(0, outer // chunk, one_chunk, 0)


def downward_kernel(
    place_ref, *refs, cells_y, cells_x, coarse_rows, coarse_cells
):
    owned = refs[:HALO_LEVELS]
    (before_ref, after_ref, packs_ref, coarse_ref, matrix_ref, up_ref, top_ref) = refs[4:11]
    near_ref, own_ref, out_ref = refs[11:14]
    scratch = list(refs[14:])
    padded, halos, fields = scratch[:4], scratch[4:8], scratch[8:12]
    stage_ref = scratch[12]
    coarse, coarse_fields = scratch[13:17], scratch[17:21]
    entry_ref = scratch[21]
    for ref in fields + coarse + coarse_fields + [entry_ref]:
        ref[...] = jnp.zeros_like(ref)
    edge = 2 * CHANNELS
    total = coarse_ref[0]
    for i in range(1, coarse_ref.shape[0]):
        total = total + coarse_ref[i]
    count = coarse_rows
    level = 0
    up = up_ref[...]
    value = total
    while True:
        coarse[level][edge : edge + count * CHANNELS, :] = value
        if count == 1:
            break
        value = jnp.concatenate(raise_level(up, value, count, 1 << level), axis=0)
        count //= 2
        level += 1
    stride = 1 << level
    steps = top_steps(coarse_cells >> level)
    if steps:
        base = coarse[level][edge : edge + PITCH, :]
        pieces = [shifted_lanes(base, 0.0, d * stride) for d in steps]
        coarse_fields[level][:PITCH, :] = jnp.dot(
            top_ref[...], jnp.concatenate(pieces, axis=0), **HIGH
        )
    while level > 0:
        level -= 1
        count *= 2
        far_rows(
            matrix_ref, coarse[level], None, count, 1 << level,
            coarse_fields[level + 1], coarse_fields[level], stage_ref,
        )
    rows_here = cells_y >> HALO_LEVELS
    width = cells_x >> HALO_LEVELS
    mine = coarse_fields[0][pl.ds(pl.multiple_of(place_ref[1] * rows_here * PITCH, 8), rows_here * PITCH), :]
    lane = lanes_of((cells_x, cells_x))
    source = lax.broadcasted_iota(jnp.int32, (cells_x, cells_x), 0)
    wanted = (source - place_ref[0] * width) * (1 << HALO_LEVELS)
    choose = ((lane == wanted) & (wanted >= 0)).astype(jnp.float32)
    entry_ref[...] = jnp.dot(mine, choose, **HIGH)
    starts = pack_starts(cells_y)
    across = []
    for i in range(3):
        across.append(packs_ref[i].T)
    for k in range(HALO_LEVELS - 1, -1, -1):
        count = cells_y >> k
        used = count * CHANNELS
        padded[k][:edge, :] = before_ref[k * edge : (k + 1) * edge, :]
        padded[k][edge : edge + used, :] = owned[k][...]
        padded[k][edge + used :, :] = after_ref[k * edge : (k + 1) * edge, :]
        which = lax.broadcasted_iota(jnp.int32, (8, cells_x), 0)
        spread = (lanes_of((8, cells_x)) == edge_lane(which, k, cells_x)).astype(jnp.float32)
        begin, end = starts[k], starts[k] + used
        halos[k][:edge, :] = jnp.dot(across[0][end - edge : end], spread, **HIGH)
        halos[k][edge : edge + used, :] = jnp.dot(across[1][begin:end], spread, **HIGH)
        halos[k][edge + used :, :] = jnp.dot(across[2][begin : begin + edge], spread, **HIGH)
        far_rows(
            matrix_ref, padded[k], halos[k], count, 1 << k,
            entry_ref if k == HALO_LEVELS - 1 else fields[k + 1], fields[k], stage_ref,
        )
    half_slots = own_ref.shape[1]
    scale = 1.0 / (2.0 * math.pi)
    for row in range(0, cells_y, BAND):
        here = pl.ds(row, BAND)

        def one_slot(t, carry):
            pos_x, pos_y = own_ref[0, t, here, :], own_ref[1, t, here, :]
            coefs = [
                fields[0][pl.ds(row * PITCH + c, BAND, stride=PITCH), :] for c in range(CHANNELS)
            ]
            real, imag = coefs[ORDER - 1], coefs[2 * ORDER - 1]
            for l in range(ORDER - 2, -1, -1):
                real, imag = (
                    real * pos_x - imag * pos_y + coefs[l],
                    real * pos_y + imag * pos_x + coefs[ORDER + l],
                )
            out_ref[0, t, here, :] = (imag + near_ref[1, t, here, :]) * scale
            out_ref[1, t, here, :] = (real + near_ref[0, t, here, :]) * scale
            return carry

        lax.fori_loop(0, half_slots, one_slot, 0)


VMEM = pl.BlockSpec(memory_space=pltpu.VMEM)
SMEM = pl.BlockSpec(memory_space=pltpu.SMEM)
PARAMS = pltpu.CompilerParams(vmem_limit_bytes=48 * 1024 * 1024)


def climb(place, own, other):
    cells_y, cells_x = own.shape[2:]
    shapes = [(CHANNELS * (cells_y >> k), cells_x) for k in range(HALO_LEVELS + 1)]
    shapes.append((8, pack_starts(cells_y)[-1]))
    return pl.pallas_call(
        upward_kernel,
        out_shape=[jax.ShapeDtypeStruct(s, jnp.float32) for s in shapes],
        in_specs=[SMEM, VMEM, VMEM, VMEM],
        out_specs=[VMEM] * len(shapes),
        compiler_params=PARAMS,
        name="climb",
    )(place, own, other, jnp.asarray(upward_matrix()))


def descend(place, owned, before, after, packs, coarse, near, own, coarse_cells):
    cells_y, cells_x = own.shape[2:]
    coarse_rows = coarse.shape[1] // CHANNELS
    levels = coarse_rows.bit_length()
    top = top_matrix(coarse_cells >> (levels - 1))
    matrix = level_matrix()
    edge = 2 * CHANNELS
    scratch = []
    for extra in range(2):
        for k in range(HALO_LEVELS):
            scratch.append((CHANNELS * (cells_y >> k) + 2 * edge, cells_x))
    for k in range(HALO_LEVELS):
        scratch.append((PITCH * (cells_y >> k), cells_x))
    scratch.append((matrix.shape[1], 4 * cells_x))
    for k in range(levels):
        scratch.append((CHANNELS * (coarse_rows >> k) + 2 * edge, cells_x))
    for k in range(levels):
        scratch.append((PITCH * max(coarse_rows >> k, 1), cells_x))
    scratch.append((PITCH * (cells_y >> HALO_LEVELS), cells_x))
    return pl.pallas_call(
        functools.partial(
            downward_kernel,
            cells_y=cells_y,
            cells_x=cells_x,
            coarse_rows=coarse_rows,
            coarse_cells=coarse_cells,
        ),
        out_shape=jax.ShapeDtypeStruct((2,) + own.shape[1:], jnp.float32),
        in_specs=[SMEM] + [VMEM] * 13,
        out_specs=VMEM,
        scratch_shapes=[pltpu.VMEM(s, jnp.float32) for s in scratch],
        compiler_params=PARAMS,
        name="descend",
    )(
        place, *owned, before, after, packs, coarse, jnp.asarray(matrix),
        jnp.asarray(upward_matrix()), jnp.asarray(top), near, own,
    )


MESH = pl.DeviceIdType.MESH


def greet(partners):
    barrier = pltpu.get_barrier_semaphore()
    count = jnp.int32(0)
    for present, device in partners:
        if present is None:
            pl.semaphore_signal(barrier, inc=1, device_id=device, device_id_type=MESH)
            count = count + 1
        else:

            @pl.when(present)
            def _():
                pl.semaphore_signal(barrier, inc=1, device_id=device, device_id_type=MESH)

            count = count + present.astype(jnp.int32)
    pl.semaphore_wait(barrier, count)


def position(offset, cells, levels, sign):
    c = lax.axis_index("cell") + sign * offset[0]
    l = lax.axis_index("level") + sign * offset[1]
    r = lax.axis_index("rep")
    r = 1 - r if offset[2] else r
    present = None
    if offset[0] or offset[1]:
        present = (c >= 0) & (c < cells) & (l >= 0) & (l < levels)
    return present, (c, l, r)


def guarded(present, action):
    if present is None:
        action()
    else:
        pl.when(present)(action)


def exchange_kernel(*refs, cells, levels, messages, inputs):
    sources, outs, (send_sem, recv_sem) = refs[:inputs], refs[inputs:-2], refs[-2:]
    offsets = sorted({offset for _, offset in messages})
    greet([position(offset, cells, levels, 1) for offset in offsets])

    def copy(i, device):
        return pltpu.make_async_remote_copy(
            src_ref=sources[messages[i][0]],
            dst_ref=outs[i],
            send_sem=send_sem.at[i],
            recv_sem=recv_sem.at[i],
            device_id=device,
            device_id_type=MESH,
        )

    for i, (_, offset) in enumerate(messages):
        present, device = position(offset, cells, levels, -1)
        guarded(present, lambda i=i, device=device: copy(i, device).start())
    for i, (_, offset) in enumerate(messages):
        present, device = position(offset, cells, levels, -1)
        guarded(present, lambda i=i, device=device: copy(i, device).wait_send())
        present, device = position(offset, cells, levels, 1)
        guarded(present, lambda i=i, device=device: copy(i, device).wait_recv())
        if present is not None:

            @pl.when(jnp.logical_not(present))
            def _(i=i):
                outs[i][...] = jnp.zeros_like(outs[i])


def exchange(arrays, messages, number, name):
    cells, levels = lax.axis_size("cell"), lax.axis_size("level")
    return pl.pallas_call(
        functools.partial(
            exchange_kernel, cells=cells, levels=levels, messages=messages, inputs=len(arrays)
        ),
        out_shape=[jax.ShapeDtypeStruct(arrays[i].shape, jnp.float32) for i, _ in messages],
        in_specs=[VMEM] * len(arrays),
        out_specs=[VMEM] * len(messages),
        scratch_shapes=[pltpu.SemaphoreType.DMA((len(messages),))] * 2,
        compiler_params=pltpu.CompilerParams(
            collective_id=number, has_side_effects=True, vmem_limit_bytes=48 * 1024 * 1024
        ),
        name=name,
    )(*arrays)


def spread_kernel(mine_ref, out_ref, send_sem, recv_sem, *, cells, levels, by_target):
    c, l, r = lax.axis_index("cell"), lax.axis_index("level"), lax.axis_index("rep")
    turns = [(i, j) for i in range(cells) for j in range(1 if by_target else levels) if i or j]

    def device(turn, sign):
        return (
            lax.rem(c + sign * turn[0] + cells, cells),
            lax.rem(l + sign * turn[1] + levels, levels),
            r,
        )

    def place(at):
        if by_target:
            return out_ref.at[at[0]]
        rows = mine_ref.shape[0]
        return out_ref.at[at[0], pl.ds(pl.multiple_of(at[1] * rows, 8), rows)]

    def copy(i, source, target):
        return pltpu.make_async_remote_copy(
            src_ref=mine_ref.at[target[0]] if by_target else mine_ref,
            dst_ref=place(source),
            send_sem=send_sem.at[i],
            recv_sem=recv_sem.at[i],
            device_id=target,
            device_id_type=MESH,
        )

    greet([(None, device(turn, 1)) for turn in turns])
    for i, turn in enumerate(turns):
        copy(i, (c, l, r), device(turn, 1)).start()
    if by_target:
        out_ref[c] = mine_ref[c]
    else:
        rows = mine_ref.shape[0]
        out_ref[c, pl.ds(pl.multiple_of(l * rows, 8), rows), :] = mine_ref[...]
    for i, turn in enumerate(turns):
        copy(i, (c, l, r), device(turn, 1)).wait_send()
        copy(i, device(turn, -1), (c, l, r)).wait_recv()


def spread(mine, number, by_target, name):
    cells, levels = lax.axis_size("cell"), lax.axis_size("level")
    shape = mine.shape if by_target else (cells, levels * mine.shape[0], mine.shape[1])
    count = cells * (1 if by_target else levels) - 1
    return pl.pallas_call(
        functools.partial(spread_kernel, cells=cells, levels=levels, by_target=by_target),
        out_shape=jax.ShapeDtypeStruct(shape, jnp.float32),
        in_specs=[VMEM],
        out_specs=VMEM,
        scratch_shapes=[pltpu.SemaphoreType.DMA((count,))] * 2,
        compiler_params=pltpu.CompilerParams(collective_id=number, has_side_effects=True),
        name=name,
    )(mine)


LANES = 128
PER_CHUNK = 8


def three_parts(value):
    high = value.astype(jnp.bfloat16).astype(jnp.float32)
    middle = (value - high).astype(jnp.bfloat16).astype(jnp.float32)
    return [high, middle, (value - high) - middle]


def one_hot_rows(index_row, rows):
    return lax.broadcasted_iota(jnp.int32, (rows, LANES), 0) == index_row


def stage_movers(a_ref, b_ref, j, row, lane, parts):
    lanes = slice(j * LANES, (j + 1) * LANES)
    a_ref[:, lanes] = jnp.where(one_hot_rows(row, a_ref.shape[0]), 1.0, 0.0).astype(jnp.bfloat16)
    at = one_hot_rows(lane, LANES)
    for p, part in enumerate(parts):
        b_ref[p * LANES : (p + 1) * LANES, lanes] = jnp.where(at, part, 0.0).astype(jnp.bfloat16)


def multiply_staged(a_ref, b_ref):
    return lax.dot_general(
        a_ref[...], b_ref[...], (((1,), (1,)), ((), ())), preferred_element_type=jnp.float32
    )


def pack_kernel(pos_ref, strength_ref, owner_ref, leaf_ref, slot_ref, out_ref, a_ref, b_ref, acc_ref, *, leaves):
    cells = out_ref.shape[0]
    owner = owner_ref[...]
    rows = owner.shape[0]
    first = lax.broadcasted_iota(jnp.int32, (LANES, LANES), 0)
    upto = jnp.where(first <= lanes_of((LANES, LANES)), 1.0, 0.0).astype(jnp.bfloat16)
    ones = jnp.ones((LANES, LANES), jnp.bfloat16)
    before = lax.broadcasted_iota(jnp.int32, (rows, rows), 0) > lanes_of((rows, rows))
    before = jnp.where(before, 1.0, 0.0).astype(jnp.bfloat16)
    dest = jnp.zeros(owner.shape, jnp.float32)
    for o in range(cells):
        mask = jnp.where(owner == o, 1.0, 0.0)
        narrow = mask.astype(jnp.bfloat16)
        inside = jnp.dot(narrow, upto, preferred_element_type=jnp.float32)
        above = jnp.dot(before, narrow, preferred_element_type=jnp.float32).astype(jnp.bfloat16)
        above = jnp.dot(above, ones, preferred_element_type=jnp.float32)
        dest = dest + mask * (inside + above + float(o * CAP - 1))
    dest = dest.astype(jnp.int32)
    address = slot_ref[...] * leaves + leaf_ref[...]
    parts = three_parts(pos_ref[0]) + three_parts(pos_ref[1]) + three_parts(strength_ref[...])
    parts.append(((address >> 8) + 1).astype(jnp.float32))
    parts.append((address & 255).astype(jnp.float32))
    to_row, to_lane = dest >> 7, dest & 127
    for chunk in range(rows // PER_CHUNK):
        for j in range(PER_CHUNK):
            row = slice(chunk * PER_CHUNK + j, chunk * PER_CHUNK + j + 1)
            stage_movers(a_ref, b_ref, j, to_row[row], to_lane[row], [p[row] for p in parts])
        product = multiply_staged(a_ref, b_ref)
        acc_ref[...] = product if chunk == 0 else acc_ref[...] + product
    for v in range(4):
        if v < 3:
            block = [acc_ref[:, (3 * v + p) * LANES : (3 * v + p + 1) * LANES] for p in range(3)]
            value = (block[0] + block[1]) + block[2]
        else:
            value = (acc_ref[:, 9 * LANES : 10 * LANES] - 1.0) * 256.0 + acc_ref[:, 10 * LANES :]
        for c in range(cells):
            out_ref[c, v * 8 : (v + 1) * 8, :] = value[c * 8 : (c + 1) * 8]


def pack_movers(pos, strength, owner, leaf, slot, leaves, cells):
    rows = strength.shape[0]
    return pl.pallas_call(
        functools.partial(pack_kernel, leaves=leaves),
        out_shape=jax.ShapeDtypeStruct((cells, 32, LANES), jnp.float32),
        in_specs=[VMEM] * 5,
        out_specs=VMEM,
        scratch_shapes=[
            pltpu.VMEM((cells * 8, PER_CHUNK * LANES), jnp.bfloat16),
            pltpu.VMEM((11 * LANES, PER_CHUNK * LANES), jnp.bfloat16),
            pltpu.VMEM((cells * 8, 11 * LANES), jnp.float32),
        ],
        compiler_params=PARAMS,
        name="pack_movers",
    )(pos, strength, owner, leaf, slot)


def settle_kernel(
    arrived_ref, pos_ref, strength_ref, out_ref, first_ref, last_ref, pack_ref, a_ref, b_ref, acc_ref
):
    half_slots, cells_y, cells_x = strength_ref.shape
    rows = half_slots * cells_y
    acc_ref[...] = jnp.zeros_like(acc_ref)

    def one_source(c, carry):
        place = arrived_ref[c, 24:32, :].astype(jnp.int32)
        to_row, to_lane = place >> 7, place & 127
        parts = []
        for v in range(3):
            parts += three_parts(arrived_ref[c, v * 8 : (v + 1) * 8, :])
        parts.append(jnp.ones_like(parts[0]))
        for j in range(PER_CHUNK):
            row = slice(j, j + 1)
            stage_movers(a_ref, b_ref, j, to_row[row], to_lane[row], [p[row] for p in parts])
        acc_ref[...] = acc_ref[...] + multiply_staged(a_ref, b_ref)
        return carry

    lax.fori_loop(0, arrived_ref.shape[0], one_source, 0)
    taken = acc_ref[:, 9 * LANES :] > 0.5
    packed = jnp.zeros(pack_ref.shape, jnp.float32)
    which = lax.broadcasted_iota(jnp.int32, (8, cells_x), 0)
    for v in range(3):
        block = [acc_ref[:, (3 * v + p) * LANES : (3 * v + p + 1) * LANES] for p in range(3)]
        old = (strength_ref[...] if v == 2 else pos_ref[v]).reshape(rows, cells_x)
        value = jnp.where(taken, (block[0] + block[1]) + block[2], old)
        out_ref[v] = value.reshape(half_slots, cells_y, cells_x)
        pick = (lanes_of((8, cells_x)) == side_lane(which, v, cells_x)).astype(jnp.float32)
        packed = packed + lax.dot_general(pick, value, (((1,), (1,)), ((), ())), **HIGH)
    pack_ref[...] = packed
    for v in range(3):
        for s in range(half_slots):
            row = v * half_slots + s
            first_ref[row : row + 1, :] = out_ref[v, s, 0:1, :]
            last_ref[row : row + 1, :] = out_ref[v, s, cells_y - 1 :, :]


def side_lane(which, v, cells_x):
    return jnp.where(which == v, 0, jnp.where(which == 4 + v, cells_x - 1, -1))


def settle(arrived, pos, strength):
    half_slots, cells_y, cells_x = strength.shape
    rows = half_slots * cells_y
    shapes = [(3,) + strength.shape, (3 * half_slots, cells_x), (3 * half_slots, cells_x), (8, rows)]
    return pl.pallas_call(
        settle_kernel,
        out_shape=[jax.ShapeDtypeStruct(s, jnp.float32) for s in shapes],
        in_specs=[VMEM] * 3,
        out_specs=[VMEM] * 4,
        scratch_shapes=[
            pltpu.VMEM((rows, PER_CHUNK * LANES), jnp.bfloat16),
            pltpu.VMEM((10 * LANES, PER_CHUNK * LANES), jnp.bfloat16),
            pltpu.VMEM((rows, 10 * LANES), jnp.float32),
        ],
        compiler_params=PARAMS,
        name="settle",
    )(arrived, pos, strength)


def near_kernel(own_ref, other_ref, before_ref, after_ref, packs_ref, out_ref, src_ref):
    half_slots, cells_y, cells_x = own_ref.shape[1:]
    slot_count = 2 * half_slots
    which = lax.broadcasted_iota(jnp.int32, (8, cells_x), 0)
    for half, ref in enumerate((own_ref, other_ref)):
        across = [packs_ref[half, i].T for i in range(3)]
        for v in range(3):
            pick = (lanes_of((8, cells_x)) == side_lane(which, v, cells_x)).astype(jnp.float32)
            halo = [jnp.dot(a, pick, **HIGH) for a in across]
            halo = [h.reshape(half_slots, cells_y, cells_x) for h in halo]
            rows = slice(v * half_slots, (v + 1) * half_slots)
            top, bottom = before_ref[half, rows, :], after_ref[half, rows, :]
            slots = slice(half * half_slots, (half + 1) * half_slots)
            for step in (-1, 0, 1):
                bias = float(step) if v == 0 else 0.0
                src_ref[step + 1, v, slots, FRONT : FRONT + cells_y, :] = (
                    shifted_lanes(ref[v], halo[1], step) + bias
                )
                up = shifted_lanes(top, halo[0][:, cells_y - 1, :], step) + bias
                down = shifted_lanes(bottom, halo[2][:, 0, :], step) + bias
                for s in range(half_slots):
                    slot = half * half_slots + s
                    src_ref[step + 1, v, slot, FRONT - 1 : FRONT, :] = up[s : s + 1]
                    src_ref[step + 1, v, slot, FRONT + cells_y : FRONT + cells_y + 1, :] = down[s : s + 1]

    def one_block(index, carry):
        row = pl.multiple_of((index // (half_slots // GROUP)) * BAND, BAND)
        slot = (index % (half_slots // GROUP)) * GROUP
        here = pl.ds(row, BAND)
        target_x = [own_ref[0, slot + t, here, :] for t in range(GROUP)]
        target_y = [own_ref[1, slot + t, here, :] for t in range(GROUP)]

        def one_source(s, sums):
            sums = list(sums)
            for step_y in (-1, 0, 1):
                there = pl.ds(row + FRONT + step_y, BAND)
                for step_x in (-1, 0, 1):
                    source_x = src_ref[step_x + 1, 0, s, there, :]
                    source_y = src_ref[step_x + 1, 1, s, there, :] + float(step_y)
                    strength = src_ref[step_x + 1, 2, s, there, :]
                    for t in range(GROUP):
                        gap_x = target_x[t] - source_x
                        gap_y = target_y[t] - source_y
                        square = gap_x * gap_x + (gap_y * gap_y + blob_square)
                        weight = strength * pl.reciprocal(square, approx=True)
                        sums[t] = sums[t] + weight * gap_x
                        sums[GROUP + t] = sums[GROUP + t] + weight * gap_y
            return tuple(sums)

        zero = jnp.zeros((BAND, cells_x), jnp.float32)
        sums = lax.fori_loop(0, slot_count, one_source, (zero,) * (2 * GROUP))
        for t in range(GROUP):
            out_ref[0, slot + t, here, :] = sums[t]
            out_ref[1, slot + t, here, :] = -sums[GROUP + t]
        return carry

    lax.fori_loop(0, (cells_y // BAND) * (half_slots // GROUP), one_block, 0)


def near_field(own, other, before, after, packs):
    half_slots, cells_y, cells_x = own.shape[1:]
    return pl.pallas_call(
        near_kernel,
        out_shape=jax.ShapeDtypeStruct((2,) + own.shape[1:], jnp.float32),
        in_specs=[VMEM] * 5,
        out_specs=VMEM,
        scratch_shapes=[
            pltpu.VMEM((3, 3, 2 * half_slots, cells_y + 2 * FRONT, cells_x), jnp.float32)
        ],
        compiler_params=PARAMS,
        name="near_field",
    )(own, other, before, after, packs)


def merged_sides(left, right):
    half = left.shape[-2] // 2
    return jnp.concatenate([right[..., :half, :], left[..., half:, :]], axis=-2)


def local(
    resident_pos, resident_strength, mover_pos, mover_strength, mover_owner, mover_leaf, mover_slot
):
    cells, levels = lax.axis_size("cell"), lax.axis_size("level")
    half_slots, cells_y, cells_x = resident_strength.shape
    place = jnp.stack([lax.axis_index("cell"), lax.axis_index("level")]).astype(jnp.int32)
    packed = pack_movers(
        mover_pos.reshape(2, -1, LANES),
        mover_strength.reshape(-1, LANES),
        mover_owner.reshape(-1, LANES),
        mover_leaf.reshape(-1, LANES),
        mover_slot.reshape(-1, LANES),
        cells_y * cells_x,
        cells,
    )
    arrived = spread(packed, 0, True, "send_movers")
    own, first, last, sides = settle(arrived, resident_pos, resident_strength)
    around = [(c, l) for l in (-1, 0, 1) for c in (-1, 1)]
    messages = [(0, (0, 0, 1))]
    for rep in (0, 1):
        messages += [(2, (0, -1, rep)), (1, (0, 1, rep))]
        messages += [(3, (c, l, rep)) for c, l in around]
    got = exchange([own, first, last, sides], messages, 1, "send_particles")
    other = got[0]
    by_rep = [got[1:9], got[9:17]]
    before = jnp.stack([g[0] for g in by_rep])
    after = jnp.stack([g[1] for g in by_rep])
    packs = jnp.stack(
        [
            jnp.stack([merged_sides(g[2 + 2 * i], g[3 + 2 * i]) for i in range(3)])
            for g in by_rep
        ]
    )
    climbed = climb(place, own, other)
    owned, mine, edges = climbed[:HALO_LEVELS], climbed[HALO_LEVELS], climbed[HALO_LEVELS + 1]
    edge = 2 * CHANNELS
    top_rows = jnp.concatenate([m[:edge] for m in owned])
    low_rows = jnp.concatenate([m[-edge:] for m in owned])
    messages = [(1, (0, -1, 0)), (0, (0, 1, 0))] + [(2, (c, l, 0)) for c, l in around]
    halo = exchange([top_rows, low_rows, edges], messages, 2, "send_multipoles")
    coarse = spread(mine, 3, False, "send_coarse")
    level_packs = jnp.stack([merged_edges(halo[2 + 2 * i], halo[3 + 2 * i]) for i in range(3)])
    near = near_field(own, other, before, after, packs)
    return descend(
        place, owned, halo[0], halo[1], level_packs, coarse, near, own,
        cells * (cells_x >> HALO_LEVELS),
    )


def merged_edges(left, right):
    return jnp.concatenate([right[:2], left[2:]], axis=0)


def solution(mesh):
    return jax.shard_map(
        local,
        mesh=mesh,
        in_specs=(
            P(None, "rep", "level", "cell"),
            P("rep", "level", "cell"),
            P(None, "rep", "level", "cell"),
            P("rep", "level", "cell"),
            P("rep", "level", "cell"),
            P("rep", "level", "cell"),
            P("rep", "level", "cell"),
        ),
        out_specs=P(None, "rep", "level", "cell"),
        check_vma=False,
    )
```

time: 853 us -> 121 us (0.14); the launches traced: 839 us -> 120 us
  local copies, waits for them, and re-layouts: 566 us -> 7.85 us
  Pallas kernels: 37.9 us -> 112 us
  starting transfers between devices: 67.7 us -> 0 us
  matrix products: 54.3 us -> 0 us
  blocking collectives: 43.1 us -> 0 us
  other arithmetic: 39.5 us -> 0.22 us
  between operations: 16.8 us -> 0.39 us
  waiting for transfers between devices: 14.3 us -> 0 us
    slice x305 -> x20, local copies, waits for them, and re-layouts: 327 us -> 0.11 us  [the longest x12 0.05 us: merged_sides(): return jnp.concatenate([right[..., :half, :], left[..., half:, :]], axis=-2)]
    concatenate x30 -> x0, local copies, waits for them, and re-layouts: 82.7 us -> none  [the longest x28 64.7 us: grouped_far(): jnp.concatenate(pieces, axis=0)]
    unnamed x199 -> x28, local copies, waits for them, and re-layouts: 85.6 us -> 7.74 us
    pallas_call x1 -> x9, Pallas kernels: 37.9 us -> 112 us  [the longest x1 35.8 us: near_field(): pl.pallas_call(near_kernel, out_shape=jax.ShapeDtypeStruct((2,) + own.sha...]
    ppermute x20 -> x0, starting transfers between devices: 56.3 us -> none  [the longest x10 43.2 us: with_halo(): before = lax.ppermute(last, axis, up)]
    all_gather x1 -> x0, blocking collectives: 43.1 us -> none  [local(): lax.all_gather(coarse_own[None], ('cell', 'level'), axis=0, tiled=True)]
    dot_general x56 -> x0, matrix products: 42 us -> none  [apply_matrix(): jnp.einsum('ij,jyx->iyx', jnp.asarray(matrix, dtype=jnp.float32), level_f...]
    scatter x2 -> x0, local copies, waits for them, and re-layouts: 35.5 us -> none  [the longest x1 32.7 us: local(): resident.at[:, arrived_at.reshape(-1)]]
  transfers between devices with their start and end apart: 23 -> 0, of which waited for: 2 -> 0; matrix products, arithmetic and copies ran while one was open for 60% -> 0% of each run, Pallas kernels for 0% -> 0%
where the time goes in v2:
time: 121 us; the launch traced here: 120 us
  Pallas kernels  112 us (93%)
  local copies, waits for them, and re-layouts  7.85 us (6%)
    pallas_call x1, Pallas kernels, near_field(): pl.pallas_call(near_kernel, out_shape=jax.ShapeDtypeStruct((2,) + own.sha...  35.8 us
    pallas_call x2, Pallas kernels, spread(): pl.pallas_call(functools.partial(spread_kernel, cells=cells, levels=level...  24.1 us
    pallas_call x2, Pallas kernels, exchange(): pl.pallas_call(functools.partial(exchange_kernel, cells=cells, levels=lev...  19.7 us
    pallas_call x1, Pallas kernels, descend(): pl.pallas_call(functools.partial(downward_kernel, cells_y=cells_y, cells_...  13.1 us
    pallas_call x1, Pallas kernels, settle(): pl.pallas_call(settle_kernel, out_shape=[jax.ShapeDtypeStruct(s, jnp.floa...  9.25 us
    unnamed x28, local copies, waits for them, and re-layouts  7.74 us
    pallas_call x1, Pallas kernels, pack_movers(): pl.pallas_call(functools.partial(pack_kernel, leaves=leaves), out_shape=j...  5.42 us
    pallas_call x1, Pallas kernels, climb(): pl.pallas_call(upward_kernel, out_shape=[jax.ShapeDtypeStruct(s, jnp.floa...  4.31 us

profile of v2, /device:TPU:0, one launch (start us, length us, event | category | flops | bytes accessed | tf_op | source)
XLA Modules:
  0.0 120.2 jit_solution(8397686497410093461)
XLA Ops:
  0.0 0.1 pad_add_fusion.place_ref
  0.1 0.8 copy-done.7
  0.9 0.7 copy-done.9
  1.6 0.7 copy-done.10
  2.3 0.7 copy-done.11
  3.0 0.7 copy-done.12
  3.7 5.4 %pack_movers.1.mine_ref = f32[4,32,128]{2,1,0:T(8,128)S(1)} custom-call(f32[2,32,128]{2,1,0:T(8,128)S(1)} %bitcast.33, f32[32,128]{1,0:T(8,128)S(1)} %bitcast.38, s32[32,128]{1,0:T(8,128)S(1)} %bitcast.39, s32[32,128]{1,0:T(8,128)S(1)} %bitcast.40, s32[32,128]{1,0:T(8,128)S(1)} %bitcast.41), custom_call_target="tpu_custom_call" | custom-call | tf_op jit(solution)/shard_map/pack_movers/pallas_call | solution.py:597
  9.2 0.0 copy-start.4
  9.2 0.6 copy-done.4
  9.8 9.1 %send_movers.1.arrived_ref = f32[4,32,128]{2,1,0:T(8,128)} custom-call(f32[4,32,128]{2,1,0:T(8,128)} %copy-done.4), custom_call_target="tpu_custom_call" | custom-call | tf_op jit(solution)/shard_map/send_movers/pallas_call | solution.py:517
  18.9 1.0 copy-done.1
  19.9 0.8 copy-done.5
  20.8 9.2 %settle.1 = (f32[3,16,32,128]{3,2,1,0:T(8,128)S(1)}, f32[48,128]{1,0:T(8,128)S(1)}, f32[48,128]{1,0:T(8,128)S(1)}, f32[8,512]{1,0:T(8,128)S(1)}) custom-call(f32[4,32,128]{2,1,0:T(8,128)S(1)} %copy-done.5, f32[2,16,32,128]{3,2,1,0:T(8,128)S(1)} %copy-done.1, f32[16,32,128]{2,1,0:T(8,128)S(1)} %copy-done.3), custom_call_target="tpu_custom_call" | custom-call | tf_op jit(solution)/shard_map/settle/pallas_call | solution.py:659
  30.0 8.0 %send_particles.1 = (f32[3,16,32,128]{3,2,1,0:T(8,128)S(1)}, f32[48,128]{1,0:T(8,128)S(1)}, f32[48,128]{1,0:T(8,128)S(1)}, f32[8,512]{1,0:T(8,128)S(1)}, f32[8,5...) custom-call(f32[3,16,32,128]{3,2,1,0:T(8,128)S(1)} %get-tuple-elemen, ...), custom_call_target="tpu_custom_call" | custom-call | tf_op jit(solution)/shard_map/send_particles/pallas_call | solution.py:458
  38.3 0.0 copy-start.6
  38.3 35.8 %near_field.1.refs_11_ = f32[2,16,32,128]{3,2,1,0:T(8,128)S(1)} custom-call(f32[3,16,32,128]{3,2,1,0:T(8,128)S(1)} %get-tuple-element.40.refs_0_.own_ref.refs_12_, f32[3,16,32,128]{3,2,1,0:T(8,128)S(1)} %get-tuple-element.44.other_ref, f32[2,48,128]{2,1,0:T(8,128)S(1)} %get-tuple-element.91.before_ref, f32[2,48,128]{2,1,0:T(8,128)S(1)} %get-tuple-element.92.after_ref, ...), custom_call_target="tpu_custom_call" | custom-call | tf_op jit(solution)/shard_map/near_field/pallas_call | solution.py:735
  74.2 4.3 %climb.1 = (f32[640,128]{1,0:T(8,128)S(1)}, f32[320,128]{1,0:T(8,128)S(1)}, f32[160,128]{1,0:T(8,128)S(1)}, f32[80,128]{1,0:T(8,128)S(1)}, f32[40,128]{1,0:T(8,128)S(1)}, /*index=5*/f32[8,1408]{1,0:T(8,128)S(1)}) custom-call(s32[2]{0:T(128)S(1)} %pad_add_fusion.place_ref, f32[3,16,32,128]{3,2,1,0:T(8,128)S(1)} %get-tuple-element.40.refs_0_.own_ref.refs_12_, ...), custom_call_target="tpu_custom_call" | custom-call | tf_op jit(solution)/shard_map/climb/pallas_call | solution.py:339
  78.5 0.6 copy-done.8
  79.1 11.7 %send_multipoles.1 = (f32[160,128]{1,0:T(8,128)S(1)}, f32[160,128]{1,0:T(8,128)S(1)}, f32[8,1408]{1,0:T(8,128)S(1)}, f32[8,1408]{1,0:T(8,128)S(1)}, f32[8,1408]{...) custom-call(f32[160,128]{1,0:T(8,128)S(1)} %pad_maximum_fusion.2.refs_0_, ...), custom_call_target="tpu_custom_call" | custom-call | tf_op jit(solution)/shard_map/send_multipoles/pallas_call | solution.py:458
  91.0 0.0 copy-start.2
  91.0 0.0 copy-start.13
  91.0 15.1 %send_coarse.1.refs_7_ = f32[4,160,128]{2,1,0:T(8,128)} custom-call(f32[40,128]{1,0:T(8,128)} %copy-done.8), custom_call_target="tpu_custom_call" | custom-call | tf_op jit(solution)/shard_map/send_coarse/pallas_call | solution.py:517
  106.1 1.0 copy-done
  107.1 13.1 %descend.1 = f32[2,16,32,128]{3,2,1,0:T(8,128)} custom-call(s32[2]{0:T(128)S(1)} %pad_add_fusion.place_ref, f32[640,128]{1,0:T(8,128)S(1)} %get-tuple-element.45.refs_0_, f32[320,128]{1,0:T(8,128)S(1)} %get-tuple-element.46.refs_1_, f32[160,128]{1,0:T(8,128)S(1)} %get-tuple-element.47.refs_2_, f32[80,128]{1,0:T(8,128)S(1)} %get-tuple-element.48.refs_3_, ...), custom_call_target="tpu_custom_call" | custom-call | tf_op jit(solution)/shard_map/descend/pallas_call | solution.py:368
  (48 shorter events, 0.3 us)
Async XLA Ops:
  0.0 18.9 %copy-start.3 = (f32[16,32,128]{2,1,0:T(8,128)S(1)}, f32[16,32,128]{2,1,0:T(8,128)}, u32[]{:S(2)}) copy-start(f32[16,32,128]{2,1,0:T(8,128)} %strength_ref.1) | copy-start | bytes 786436
  0.1 0.8 copy-start.7
  0.9 0.7 copy-start.9
  1.6 0.7 copy-start.10
  2.3 0.7 copy-start.11
  3.0 0.7 copy-start.12
  9.2 0.6 copy-start.4
  18.9 1.0 copy-start.1
  19.9 0.8 copy-start.5
  38.3 35.8 %copy-start.6 = (f32[24,80]{1,0:T(8,128)S(1)}, f32[24,80]{1,0:T(8,128)}, u32[]{:S(2)}) copy-start(f32[24,80]{1,0:T(8,128)} %constant.15.clone.up_ref.refs_9_) | copy-start | bytes 23044
  78.5 0.6 copy-start.8
  91.0 15.1 %copy-start.2 = (bf16[160,888]{1,0:T(8,128)(2,1)S(1)}, bf16[160,888]{1,0:T(8,128)(2,1)}, u32[]{:S(2)}) copy-start(bf16[160,888]{1,0:T(8,128)(2,1)} %constant.16.clone.refs_8_) | copy-start | bytes 852484
  91.0 15.1 %copy-start.13 = (f32[24,96]{1,0:T(8,128)S(1)}, f32[24,96]{1,0:T(8,128)}, u32[]{:S(2)}) copy-start(f32[24,96]{1,0:T(8,128)} %constant.17.clone.refs_10_) | copy-start | bytes 27652
  106.1 1.0 copy-start

commit v3 on v2

--- a/solution.py
+++ b/solution.py
@@ -132,7 +132,7 @@
     return [product[:CHANNELS, wide * row : wide * (row + 1)] for row in range(cells_y // 2)]
 
 
-def upward_kernel(place_ref, own_ref, other_ref, up_ref, zero_ref, one_ref, two_ref, three_ref, four_ref, pack_ref):
+def climb_into(own_ref, other_ref, up_ref, zero_ref, one_ref, two_ref, three_ref, four_ref, pack_ref):
     slots, cells_y, cells_x = own_ref.shape[1:]
     levels = [zero_ref, one_ref, two_ref, three_ref]
     for row in range(0, cells_y, BAND):
@@ -167,7 +167,7 @@
             lane = lanes_of((cells_x, cells_x))
             source = lax.broadcasted_iota(jnp.int32, (cells_x, cells_x), 0)
             width = cells_x >> HALO_LEVELS
-            wanted = (lane - place_ref[0] * width) * (1 << HALO_LEVELS)
+            wanted = (lane - lax.axis_index("cell") * width) * (1 << HALO_LEVELS)
             choose = ((source == wanted) & (wanted >= 0)).astype(jnp.float32)
             four = jnp.concatenate(raised, axis=0)
             four_ref[...] = jnp.dot(four, choose, **HIGH)
@@ -237,9 +237,9 @@
     place_ref, *refs, cells_y, cells_x, coarse_rows, coarse_cells
 ):
     owned = refs[:HALO_LEVELS]
-    (before_ref, after_ref, packs_ref, coarse_ref, matrix_ref, up_ref, top_ref) = refs[4:11]
-    near_ref, own_ref, out_ref = refs[11:14]
-    scratch = list(refs[14:])
+    before_ref, after_ref, sides = refs[4], refs[5], refs[6:12]
+    coarse_ref, matrix_ref, up_ref, top_ref, near_ref, own_ref, out_ref = refs[12:19]
+    scratch = list(refs[19:])
     padded, halos, fields = scratch[:4], scratch[4:8], scratch[8:12]
     stage_ref = scratch[12]
     coarse, coarse_fields = scratch[13:17], scratch[17:21]
@@ -287,7 +287,7 @@
     starts = pack_starts(cells_y)
     across = []
     for i in range(3):
-        across.append(packs_ref[i].T)
+        across.append(merged_sides(sides[2 * i], sides[2 * i + 1], 2))
     for k in range(HALO_LEVELS - 1, -1, -1):
         count = cells_y >> k
         used = count * CHANNELS
@@ -332,21 +332,7 @@
 PARAMS = pltpu.CompilerParams(vmem_limit_bytes=48 * 1024 * 1024)
 
 
-def climb(place, own, other):
-    cells_y, cells_x = own.shape[2:]
-    shapes = [(CHANNELS * (cells_y >> k), cells_x) for k in range(HALO_LEVELS + 1)]
-    shapes.append((8, pack_starts(cells_y)[-1]))
-    return pl.pallas_call(
-        upward_kernel,
-        out_shape=[jax.ShapeDtypeStruct(s, jnp.float32) for s in shapes],
-        in_specs=[SMEM, VMEM, VMEM, VMEM],
-        out_specs=[VMEM] * len(shapes),
-        compiler_params=PARAMS,
-        name="climb",
-    )(place, own, other, jnp.asarray(upward_matrix()))
-
-
-def descend(place, owned, before, after, packs, coarse, near, own, coarse_cells):
+def descend(place, owned, halo, coarse, near, own, coarse_cells):
     cells_y, cells_x = own.shape[2:]
     coarse_rows = coarse.shape[1] // CHANNELS
     levels = coarse_rows.bit_length()
@@ -374,35 +360,18 @@
             coarse_cells=coarse_cells,
         ),
         out_shape=jax.ShapeDtypeStruct((2,) + own.shape[1:], jnp.float32),
-        in_specs=[SMEM] + [VMEM] * 13,
+        in_specs=[SMEM] + [VMEM] * 18,
         out_specs=VMEM,
         scratch_shapes=[pltpu.VMEM(s, jnp.float32) for s in scratch],
         compiler_params=PARAMS,
         name="descend",
     )(
-        place, *owned, before, after, packs, coarse, jnp.asarray(matrix),
+        place, *owned, *halo, coarse, jnp.asarray(matrix),
         jnp.asarray(upward_matrix()), jnp.asarray(top), near, own,
     )
 
 
 MESH = pl.DeviceIdType.MESH
-
-
-def greet(partners):
-    barrier = pltpu.get_barrier_semaphore()
-    count = jnp.int32(0)
-    for present, device in partners:
-        if present is None:
-            pl.semaphore_signal(barrier, inc=1, device_id=device, device_id_type=MESH)
-            count = count + 1
-        else:
-
-            @pl.when(present)
-            def _():
-                pl.semaphore_signal(barrier, inc=1, device_id=device, device_id_type=MESH)
-
-            count = count + present.astype(jnp.int32)
-    pl.semaphore_wait(barrier, count)
 
 
 def position(offset, cells, levels, sign):
@@ -416,6 +385,14 @@
     return present, (c, l, r)
 
 
+def turned(turn, cells, levels, sign):
+    return (
+        lax.rem(lax.axis_index("cell") + sign * turn[0] + cells, cells),
+        lax.rem(lax.axis_index("level") + sign * turn[1] + levels, levels),
+        lax.axis_index("rep"),
+    )
+
+
 def guarded(present, action):
     if present is None:
         action()
@@ -423,106 +400,54 @@
         pl.when(present)(action)
 
 
-def exchange_kernel(*refs, cells, levels, messages, inputs):
-    sources, outs, (send_sem, recv_sem) = refs[:inputs], refs[inputs:-2], refs[-2:]
-    offsets = sorted({offset for _, offset in messages})
-    greet([position(offset, cells, levels, 1) for offset in offsets])
-
-    def copy(i, device):
+def greet(partners):
+    barrier = pltpu.get_barrier_semaphore()
+    count = jnp.int32(0)
+    for present, device in partners:
+
+        def signal(device=device):
+            pl.semaphore_signal(barrier, inc=1, device_id=device, device_id_type=MESH)
+
+        guarded(present, signal)
+        count = count + (1 if present is None else present.astype(jnp.int32))
+    return lambda: pl.semaphore_wait(barrier, count)
+
+
+class Exchange:
+    def __init__(self, sources, outs, offsets, send_sem, recv_sem, cells, levels):
+        self.sources, self.outs, self.offsets = sources, outs, offsets
+        self.send_sem, self.recv_sem = send_sem, recv_sem
+        self.grid = (cells, levels)
+
+    def copy(self, i, device):
         return pltpu.make_async_remote_copy(
-            src_ref=sources[messages[i][0]],
-            dst_ref=outs[i],
-            send_sem=send_sem.at[i],
-            recv_sem=recv_sem.at[i],
+            src_ref=self.sources[i],
+            dst_ref=self.outs[i],
+            send_sem=self.send_sem.at[i],
+            recv_sem=self.recv_sem.at[i],
             device_id=device,
             device_id_type=MESH,
         )
 
-    for i, (_, offset) in enumerate(messages):
-        present, device = position(offset, cells, levels, -1)
-        guarded(present, lambda i=i, device=device: copy(i, device).start())
-    for i, (_, offset) in enumerate(messages):
-        present, device = position(offset, cells, levels, -1)
-        guarded(present, lambda i=i, device=device: copy(i, device).wait_send())
-        present, device = position(offset, cells, levels, 1)
-        guarded(present, lambda i=i, device=device: copy(i, device).wait_recv())
-        if present is not None:
-
-            @pl.when(jnp.logical_not(present))
-            def _(i=i):
-                outs[i][...] = jnp.zeros_like(outs[i])
-
-
-def exchange(arrays, messages, number, name):
-    cells, levels = lax.axis_size("cell"), lax.axis_size("level")
-    return pl.pallas_call(
-        functools.partial(
-            exchange_kernel, cells=cells, levels=levels, messages=messages, inputs=len(arrays)
-        ),
-        out_shape=[jax.ShapeDtypeStruct(arrays[i].shape, jnp.float32) for i, _ in messages],
-        in_specs=[VMEM] * len(arrays),
-        out_specs=[VMEM] * len(messages),
-        scratch_shapes=[pltpu.SemaphoreType.DMA((len(messages),))] * 2,
-        compiler_params=pltpu.CompilerParams(
-            collective_id=number, has_side_effects=True, vmem_limit_bytes=48 * 1024 * 1024
-        ),
-        name=name,
-    )(*arrays)
-
-
-def spread_kernel(mine_ref, out_ref, send_sem, recv_sem, *, cells, levels, by_target):
-    c, l, r = lax.axis_index("cell"), lax.axis_index("level"), lax.axis_index("rep")
-    turns = [(i, j) for i in range(cells) for j in range(1 if by_target else levels) if i or j]
-
-    def device(turn, sign):
-        return (
-            lax.rem(c + sign * turn[0] + cells, cells),
-            lax.rem(l + sign * turn[1] + levels, levels),
-            r,
-        )
-
-    def place(at):
-        if by_target:
-            return out_ref.at[at[0]]
-        rows = mine_ref.shape[0]
-        return out_ref.at[at[0], pl.ds(pl.multiple_of(at[1] * rows, 8), rows)]
-
-    def copy(i, source, target):
-        return pltpu.make_async_remote_copy(
-            src_ref=mine_ref.at[target[0]] if by_target else mine_ref,
-            dst_ref=place(source),
-            send_sem=send_sem.at[i],
-            recv_sem=recv_sem.at[i],
-            device_id=target,
-            device_id_type=MESH,
-        )
-
-    greet([(None, device(turn, 1)) for turn in turns])
-    for i, turn in enumerate(turns):
-        copy(i, (c, l, r), device(turn, 1)).start()
-    if by_target:
-        out_ref[c] = mine_ref[c]
-    else:
-        rows = mine_ref.shape[0]
-        out_ref[c, pl.ds(pl.multiple_of(l * rows, 8), rows), :] = mine_ref[...]
-    for i, turn in enumerate(turns):
-        copy(i, (c, l, r), device(turn, 1)).wait_send()
-        copy(i, device(turn, -1), (c, l, r)).wait_recv()
-
-
-def spread(mine, number, by_target, name):
-    cells, levels = lax.axis_size("cell"), lax.axis_size("level")
-    shape = mine.shape if by_target else (cells, levels * mine.shape[0], mine.shape[1])
-    count = cells * (1 if by_target else levels) - 1
-    return pl.pallas_call(
-        functools.partial(spread_kernel, cells=cells, levels=levels, by_target=by_target),
-        out_shape=jax.ShapeDtypeStruct(shape, jnp.float32),
-        in_specs=[VMEM],
-        out_specs=VMEM,
-        scratch_shapes=[pltpu.SemaphoreType.DMA((count,))] * 2,
-        compiler_params=pltpu.CompilerParams(collective_id=number, has_side_effects=True),
-        name=name,
-    )(mine)
+    def start(self):
+        for i, offset in enumerate(self.offsets):
+            present, device = position(offset, *self.grid, -1)
+            guarded(present, lambda i=i, device=device: self.copy(i, device).start())
+
+    def wait(self):
+        for i, offset in enumerate(self.offsets):
+            present, device = position(offset, *self.grid, -1)
+            guarded(present, lambda i=i, device=device: self.copy(i, device).wait_send())
+            present, device = position(offset, *self.grid, 1)
+            guarded(present, lambda i=i, device=device: self.copy(i, device).wait_recv())
+            if present is not None:
+
+                @pl.when(jnp.logical_not(present))
+                def _(i=i):
+                    self.outs[i][...] = jnp.zeros_like(self.outs[i])
+
+
+AROUND = [(c, l) for l in (-1, 0, 1) for c in (-1, 1)]
 
 
 LANES = 128
@@ -553,8 +478,8 @@
     )
 
 
-def pack_kernel(pos_ref, strength_ref, owner_ref, leaf_ref, slot_ref, out_ref, a_ref, b_ref, acc_ref, *, leaves):
-    cells = out_ref.shape[0]
+def pack_into(packed_ref, pos_ref, strength_ref, owner_ref, leaf_ref, slot_ref, a_ref, b_ref, acc_ref, leaves):
+    cells = packed_ref.shape[0]
     owner = owner_ref[...]
     rows = owner.shape[0]
     first = lax.broadcasted_iota(jnp.int32, (LANES, LANES), 0)
@@ -589,47 +514,25 @@
         else:
             value = (acc_ref[:, 9 * LANES : 10 * LANES] - 1.0) * 256.0 + acc_ref[:, 10 * LANES :]
         for c in range(cells):
-            out_ref[c, v * 8 : (v + 1) * 8, :] = value[c * 8 : (c + 1) * 8]
-
-
-def pack_movers(pos, strength, owner, leaf, slot, leaves, cells):
-    rows = strength.shape[0]
-    return pl.pallas_call(
-        functools.partial(pack_kernel, leaves=leaves),
-        out_shape=jax.ShapeDtypeStruct((cells, 32, LANES), jnp.float32),
-        in_specs=[VMEM] * 5,
-        out_specs=VMEM,
-        scratch_shapes=[
-            pltpu.VMEM((cells * 8, PER_CHUNK * LANES), jnp.bfloat16),
-            pltpu.VMEM((11 * LANES, PER_CHUNK * LANES), jnp.bfloat16),
-            pltpu.VMEM((cells * 8, 11 * LANES), jnp.float32),
-        ],
-        compiler_params=PARAMS,
-        name="pack_movers",
-    )(pos, strength, owner, leaf, slot)
-
-
-def settle_kernel(
-    arrived_ref, pos_ref, strength_ref, out_ref, first_ref, last_ref, pack_ref, a_ref, b_ref, acc_ref
-):
+            packed_ref[c, v * 8 : (v + 1) * 8, :] = value[c * 8 : (c + 1) * 8]
+
+
+def settle_chunk(arrived, a_ref, b_ref, acc_ref):
+    place = arrived[24:32, :].astype(jnp.int32)
+    to_row, to_lane = place >> 7, place & 127
+    parts = []
+    for v in range(3):
+        parts += three_parts(arrived[v * 8 : (v + 1) * 8, :])
+    parts.append(jnp.ones_like(parts[0]))
+    for j in range(PER_CHUNK):
+        row = slice(j, j + 1)
+        stage_movers(a_ref, b_ref, j, to_row[row], to_lane[row], [p[row] for p in parts])
+    acc_ref[...] = acc_ref[...] + multiply_staged(a_ref, b_ref)
+
+
+def finish_settle(pos_ref, strength_ref, out_ref, first_ref, last_ref, pack_ref, acc_ref):
     half_slots, cells_y, cells_x = strength_ref.shape
     rows = half_slots * cells_y
-    acc_ref[...] = jnp.zeros_like(acc_ref)
-
-    def one_source(c, carry):
-        place = arrived_ref[c, 24:32, :].astype(jnp.int32)
-        to_row, to_lane = place >> 7, place & 127
-        parts = []
-        for v in range(3):
-            parts += three_parts(arrived_ref[c, v * 8 : (v + 1) * 8, :])
-        parts.append(jnp.ones_like(parts[0]))
-        for j in range(PER_CHUNK):
-            row = slice(j, j + 1)
-            stage_movers(a_ref, b_ref, j, to_row[row], to_lane[row], [p[row] for p in parts])
-        acc_ref[...] = acc_ref[...] + multiply_staged(a_ref, b_ref)
-        return carry
-
-    lax.fori_loop(0, arrived_ref.shape[0], one_source, 0)
     taken = acc_ref[:, 9 * LANES :] > 0.5
     packed = jnp.zeros(pack_ref.shape, jnp.float32)
     which = lax.broadcasted_iota(jnp.int32, (8, cells_x), 0)
@@ -648,41 +551,134 @@
             last_ref[row : row + 1, :] = out_ref[v, s, cells_y - 1 :, :]
 
 
+def particle_offsets():
+    offsets = [(0, 0, 1)]
+    for rep in (0, 1):
+        offsets += [(0, -1, rep), (0, 1, rep)] + [(c, l, rep) for c, l in AROUND]
+    return offsets
+
+
+def route_kernel(*refs, leaves, cells, levels):
+    inputs, refs = refs[:7], refs[7:]
+    own_ref, received, refs = refs[0], refs[1:18], refs[18:]
+    held, refs = refs[:7], refs[7:]
+    (
+        packed_ref, arrived_ref, a_pack, b_pack, acc_pack, a_ref, b_ref, acc_ref,
+        first_ref, last_ref, side_ref, load_sem, move_send, move_recv, send_sem, recv_sem,
+    ) = refs
+    offsets = particle_offsets()
+    partners = [(None, turned((i, 0), cells, levels, 1)) for i in range(1, cells)]
+    partners += [position(o, cells, levels, 1) for o in offsets if o[1] or o[2]]
+    all_in = greet(partners)
+    loads = [
+        pltpu.make_async_copy(source, target, load_sem.at[i])
+        for i, (source, target) in enumerate(zip(inputs, held))
+    ]
+    for load in loads:
+        load.start()
+    for load in loads[:5]:
+        load.wait()
+    pos_ref, strength_ref = held[5:]
+    pack_into(packed_ref, *held[:5], a_pack, b_pack, acc_pack, leaves)
+    acc_ref[...] = jnp.zeros_like(acc_ref)
+    me = lax.axis_index("cell")
+    all_in()
+
+    def move(i):
+        target = turned((i, 0), cells, levels, 1)
+        return pltpu.make_async_remote_copy(
+            src_ref=packed_ref.at[target[0]],
+            dst_ref=arrived_ref.at[i],
+            send_sem=move_send.at[i],
+            recv_sem=move_recv.at[i],
+            device_id=target,
+            device_id_type=MESH,
+        )
+
+    for i in range(1, cells):
+        move(i).start()
+    arrived_ref[0] = packed_ref[me]
+    settle_chunk(arrived_ref[0], a_ref, b_ref, acc_ref)
+
+    def one_source(i, carry):
+        move(i).wait_recv()
+        settle_chunk(arrived_ref[i], a_ref, b_ref, acc_ref)
+        return carry
+
+    lax.fori_loop(1, cells, one_source, 0)
+    for load in loads[5:]:
+        load.wait()
+    finish_settle(pos_ref, strength_ref, own_ref, first_ref, last_ref, side_ref, acc_ref)
+    sources = [own_ref] + [last_ref, first_ref] + [side_ref] * 6 + [last_ref, first_ref] + [side_ref] * 6
+    swap = Exchange(sources, received, offsets, send_sem, recv_sem, cells, levels)
+    swap.start()
+    for i in range(1, cells):
+        move(i).wait_send()
+    swap.wait()
+
+
+def route(movers, pos, strength):
+    cells, levels = lax.axis_size("cell"), lax.axis_size("level")
+    half_slots, cells_y, cells_x = strength.shape
+    rows = half_slots * cells_y
+    own = (3,) + strength.shape
+    edge, side = (3 * half_slots, cells_x), (8, rows)
+    shapes = [own, own] + ([edge] * 2 + [side] * 6) * 2
+    inputs = list(movers) + [pos, strength]
+    wide = PER_CHUNK * LANES
+    return pl.pallas_call(
+        functools.partial(route_kernel, leaves=cells_y * cells_x, cells=cells, levels=levels),
+        out_shape=[jax.ShapeDtypeStruct(s, jnp.float32) for s in shapes],
+        in_specs=[pl.BlockSpec(memory_space=pl.ANY)] * len(inputs),
+        out_specs=[VMEM] * len(shapes),
+        scratch_shapes=[pltpu.VMEM(x.shape, x.dtype) for x in inputs]
+        + [
+            pltpu.VMEM((cells, 32, LANES), jnp.float32),
+            pltpu.VMEM((cells, 32, LANES), jnp.float32),
+            pltpu.VMEM((cells * 8, wide), jnp.bfloat16),
+            pltpu.VMEM((11 * LANES, wide), jnp.bfloat16),
+            pltpu.VMEM((cells * 8, 11 * LANES), jnp.float32),
+            pltpu.VMEM((rows, wide), jnp.bfloat16),
+            pltpu.VMEM((10 * LANES, wide), jnp.bfloat16),
+            pltpu.VMEM((rows, 10 * LANES), jnp.float32),
+            pltpu.VMEM(edge, jnp.float32),
+            pltpu.VMEM(edge, jnp.float32),
+            pltpu.VMEM(side, jnp.float32),
+            pltpu.SemaphoreType.DMA((7,)),
+            pltpu.SemaphoreType.DMA((cells,)),
+            pltpu.SemaphoreType.DMA((cells,)),
+            pltpu.SemaphoreType.DMA((17,)),
+            pltpu.SemaphoreType.DMA((17,)),
+        ],
+        compiler_params=pltpu.CompilerParams(
+            collective_id=0, has_side_effects=True, vmem_limit_bytes=56 * 1024 * 1024
+        ),
+        name="route",
+    )(*inputs)
+
+
 def side_lane(which, v, cells_x):
     return jnp.where(which == v, 0, jnp.where(which == 4 + v, cells_x - 1, -1))
 
 
-def settle(arrived, pos, strength):
-    half_slots, cells_y, cells_x = strength.shape
-    rows = half_slots * cells_y
-    shapes = [(3,) + strength.shape, (3 * half_slots, cells_x), (3 * half_slots, cells_x), (8, rows)]
-    return pl.pallas_call(
-        settle_kernel,
-        out_shape=[jax.ShapeDtypeStruct(s, jnp.float32) for s in shapes],
-        in_specs=[VMEM] * 3,
-        out_specs=[VMEM] * 4,
-        scratch_shapes=[
-            pltpu.VMEM((rows, PER_CHUNK * LANES), jnp.bfloat16),
-            pltpu.VMEM((10 * LANES, PER_CHUNK * LANES), jnp.bfloat16),
-            pltpu.VMEM((rows, 10 * LANES), jnp.float32),
-        ],
-        compiler_params=PARAMS,
-        name="settle",
-    )(arrived, pos, strength)
-
-
-def near_kernel(own_ref, other_ref, before_ref, after_ref, packs_ref, out_ref, src_ref):
+def merged_sides(left_ref, right_ref, split):
+    row = lax.broadcasted_iota(jnp.int32, left_ref.shape, 0)
+    return jnp.where(row < split, right_ref[...], left_ref[...]).T
+
+
+def near_into(out_ref, own_ref, other_ref, frames, src_ref):
     half_slots, cells_y, cells_x = own_ref.shape[1:]
     slot_count = 2 * half_slots
     which = lax.broadcasted_iota(jnp.int32, (8, cells_x), 0)
     for half, ref in enumerate((own_ref, other_ref)):
-        across = [packs_ref[half, i].T for i in range(3)]
+        before_ref, after_ref, sides = frames[half][0], frames[half][1], frames[half][2:]
+        across = [merged_sides(sides[2 * i], sides[2 * i + 1], 4) for i in range(3)]
         for v in range(3):
             pick = (lanes_of((8, cells_x)) == side_lane(which, v, cells_x)).astype(jnp.float32)
             halo = [jnp.dot(a, pick, **HIGH) for a in across]
             halo = [h.reshape(half_slots, cells_y, cells_x) for h in halo]
             rows = slice(v * half_slots, (v + 1) * half_slots)
-            top, bottom = before_ref[half, rows, :], after_ref[half, rows, :]
+            top, bottom = before_ref[rows, :], after_ref[rows, :]
             slots = slice(half * half_slots, (half + 1) * half_slots)
             for step in (-1, 0, 1):
                 bias = float(step) if v == 0 else 0.0
@@ -730,77 +726,102 @@
     lax.fori_loop(0, (cells_y // BAND) * (half_slots // GROUP), one_block, 0)
 
 
-def near_field(own, other, before, after, packs):
+def climb_kernel(*refs, cells, levels):
+    own_ref, other_ref, refs = refs[0], refs[1], refs[2:]
+    frames, refs = [refs[:8], refs[8:16]], refs[16:]
+    up_ref, refs = refs[0], refs[1:]
+    owned, refs = refs[:HALO_LEVELS], refs[HALO_LEVELS:]
+    received, coarse_ref, near_ref, refs = refs[:8], refs[8], refs[9], refs[10:]
+    mine_ref, edges_ref, top_ref, low_ref, src_ref = refs[:5]
+    send_sem, recv_sem, coarse_send, coarse_recv = refs[5:]
+    turns = [(i, j) for i in range(cells) for j in range(levels) if i or j]
+    all_in = greet([(None, turned(turn, cells, levels, 1)) for turn in turns])
+    climb_into(own_ref, other_ref, up_ref, *owned, mine_ref, edges_ref)
+    edge = 2 * CHANNELS
+    for k in range(HALO_LEVELS):
+        here = slice(k * edge, (k + 1) * edge)
+        top_ref[here, :] = owned[k][:edge, :]
+        low_ref[here, :] = owned[k][owned[k].shape[0] - edge :, :]
+    offsets = [(0, -1, 0), (0, 1, 0)] + [(c, l, 0) for c, l in AROUND]
+    sources = [low_ref, top_ref] + [edges_ref] * 6
+    swap = Exchange(sources, received, offsets, send_sem, recv_sem, cells, levels)
+    rows = mine_ref.shape[0]
+
+    def copy(i, source, target):
+        return pltpu.make_async_remote_copy(
+            src_ref=mine_ref,
+            dst_ref=coarse_ref.at[source[0], pl.ds(pl.multiple_of(source[1] * rows, 8), rows)],
+            send_sem=coarse_send.at[i],
+            recv_sem=coarse_recv.at[i],
+            device_id=target,
+            device_id_type=MESH,
+        )
+
+    me = turned((0, 0), cells, levels, 1)
+    all_in()
+    swap.start()
+    for i, turn in enumerate(turns):
+        copy(i, me, turned(turn, cells, levels, 1)).start()
+    coarse_ref[me[0], pl.ds(pl.multiple_of(me[1] * rows, 8), rows), :] = mine_ref[...]
+    near_into(near_ref, own_ref, other_ref, frames, src_ref)
+    swap.wait()
+    for i, turn in enumerate(turns):
+        copy(i, me, turned(turn, cells, levels, 1)).wait_send()
+        copy(i, turned(turn, cells, levels, -1), me).wait_recv()
+
+
+def climb_and_near(own, other, frames):
+    cells, levels = lax.axis_size("cell"), lax.axis_size("level")
     half_slots, cells_y, cells_x = own.shape[1:]
+    owned = [(CHANNELS * (cells_y >> k), cells_x) for k in range(HALO_LEVELS)]
+    mine = (CHANNELS * (cells_y >> HALO_LEVELS), cells_x)
+    edges = (8, pack_starts(cells_y)[-1])
+    rows = (2 * CHANNELS * HALO_LEVELS, cells_x)
+    shapes = owned + [rows] * 2 + [edges] * 6
+    shapes += [(cells, levels * mine[0], cells_x), (2,) + own.shape[1:]]
+    inputs = [own, other, *frames, jnp.asarray(upward_matrix())]
     return pl.pallas_call(
-        near_kernel,
-        out_shape=jax.ShapeDtypeStruct((2,) + own.shape[1:], jnp.float32),
-        in_specs=[VMEM] * 5,
-        out_specs=VMEM,
+        functools.partial(climb_kernel, cells=cells, levels=levels),
+        out_shape=[jax.ShapeDtypeStruct(s, jnp.float32) for s in shapes],
+        in_specs=[VMEM] * len(inputs),
+        out_specs=[VMEM] * len(shapes),
         scratch_shapes=[
-            pltpu.VMEM((3, 3, 2 * half_slots, cells_y + 2 * FRONT, cells_x), jnp.float32)
+            pltpu.VMEM(mine, jnp.float32),
+            pltpu.VMEM(edges, jnp.float32),
+            pltpu.VMEM(rows, jnp.float32),
+            pltpu.VMEM(rows, jnp.float32),
+            pltpu.VMEM((3, 3, 2 * half_slots, cells_y + 2 * FRONT, cells_x), jnp.float32),
+            pltpu.SemaphoreType.DMA((8,)),
+            pltpu.SemaphoreType.DMA((8,)),
+            pltpu.SemaphoreType.DMA((cells * levels - 1,)),
+            pltpu.SemaphoreType.DMA((cells * levels - 1,)),
         ],
-        compiler_params=PARAMS,
-        name="near_field",
-    )(own, other, before, after, packs)
-
-
-def merged_sides(left, right):
-    half = left.shape[-2] // 2
-    return jnp.concatenate([right[..., :half, :], left[..., half:, :]], axis=-2)
+        compiler_params=pltpu.CompilerParams(
+            collective_id=1, has_side_effects=True, vmem_limit_bytes=48 * 1024 * 1024
+        ),
+        name="climb_and_near",
+    )(*inputs)
 
 
 def local(
     resident_pos, resident_strength, mover_pos, mover_strength, mover_owner, mover_leaf, mover_slot
 ):
-    cells, levels = lax.axis_size("cell"), lax.axis_size("level")
-    half_slots, cells_y, cells_x = resident_strength.shape
+    cells = lax.axis_size("cell")
+    cells_x = resident_strength.shape[2]
     place = jnp.stack([lax.axis_index("cell"), lax.axis_index("level")]).astype(jnp.int32)
-    packed = pack_movers(
+    movers = [
         mover_pos.reshape(2, -1, LANES),
         mover_strength.reshape(-1, LANES),
         mover_owner.reshape(-1, LANES),
         mover_leaf.reshape(-1, LANES),
         mover_slot.reshape(-1, LANES),
-        cells_y * cells_x,
-        cells,
+    ]
+    own, other, *frames = route(movers, resident_pos, resident_strength)
+    got = climb_and_near(own, other, frames)
+    owned, got = got[:HALO_LEVELS], got[HALO_LEVELS:]
+    return descend(
+        place, owned, got[:8], got[8], got[9], own, cells * (cells_x >> HALO_LEVELS)
     )
-    arrived = spread(packed, 0, True, "send_movers")
-    own, first, last, sides = settle(arrived, resident_pos, resident_strength)
-    around = [(c, l) for l in (-1, 0, 1) for c in (-1, 1)]
-    messages = [(0, (0, 0, 1))]
-    for rep in (0, 1):
-        messages += [(2, (0, -1, rep)), (1, (0, 1, rep))]
-        messages += [(3, (c, l, rep)) for c, l in around]
-    got = exchange([own, first, last, sides], messages, 1, "send_particles")
-    other = got[0]
-    by_rep = [got[1:9], got[9:17]]
-    before = jnp.stack([g[0] for g in by_rep])
-    after = jnp.stack([g[1] for g in by_rep])
-    packs = jnp.stack(
-        [
-            jnp.stack([merged_sides(g[2 + 2 * i], g[3 + 2 * i]) for i in range(3)])
-            for g in by_rep
-        ]
-    )
-    climbed = climb(place, own, other)
-    owned, mine, edges = climbed[:HALO_LEVELS], climbed[HALO_LEVELS], climbed[HALO_LEVELS + 1]
-    edge = 2 * CHANNELS
-    top_rows = jnp.concatenate([m[:edge] for m in owned])
-    low_rows = jnp.concatenate([m[-edge:] for m in owned])
-    messages = [(1, (0, -1, 0)), (0, (0, 1, 0))] + [(2, (c, l, 0)) for c, l in around]
-    halo = exchange([top_rows, low_rows, edges], messages, 2, "send_multipoles")
-    coarse = spread(mine, 3, False, "send_coarse")
-    level_packs = jnp.stack([merged_edges(halo[2 + 2 * i], halo[3 + 2 * i]) for i in range(3)])
-    near = near_field(own, other, before, after, packs)
-    return descend(
-        place, owned, halo[0], halo[1], level_packs, coarse, near, own,
-        cells * (cells_x >> HALO_LEVELS),
-    )
-
-
-def merged_edges(left, right):
-    return jnp.concatenate([right[:2], left[2:]], axis=0)
 
 
 def solution(mesh):

time: 121 us -> 95.1 us (0.79)
  Pallas kernels: 112 us -> 79.2 us
  local copies, waits for them, and re-layouts: 7.85 us -> 14.4 us
    pallas_call x8 -> x2, Pallas kernels: 98.6 us -> 66.1 us  [the longest x1 40.3 us: climb_and_near(): pl.pallas_call(functools.partial(climb_kernel, cells=cells, levels=levels...]
    unnamed x28 -> x44, local copies, waits for them, and re-layouts: 7.74 us -> 14.4 us
where the time goes in v3:
time: 95.1 us; the launch traced here: 93.8 us
  Pallas kernels  79.2 us (83%)
  local copies, waits for them, and re-layouts  14.4 us (15%)
    pallas_call x1, Pallas kernels, climb_and_near(): pl.pallas_call(functools.partial(climb_kernel, cells=cells, levels=levels...  40.3 us
    pallas_call x1, Pallas kernels, route(): pl.pallas_call(functools.partial(route_kernel, leaves=cells_y * cells_x,...  25.9 us
    unnamed x44, local copies, waits for them, and re-layouts  14.4 us
    pallas_call x1, Pallas kernels, descend(): pl.pallas_call(functools.partial(downward_kernel, cells_y=cells_y, cells_...  13 us

profile of v3, /device:TPU:0, one launch (start us, length us, event | category | flops | bytes accessed | tf_op | source)
XLA Modules:
  0.0 93.8 jit_solution(14983528949708072042)
XLA Ops:
  0.0 25.9 %route.1 = (f32[3,16,32,128]{3,2,1,0:T(8,128)}, f32[3,16,32,128]{3,2,1,0:T(8,128)}, f32[48,128]{1,0:T(8,128)}, f32[48,128]{1,0:T(8,128)}, f32[8,512]{1,0:T(8,128...) custom-call(f32[2,32,128]{2,1,0:T(8,128)} %bitcast.7, ...), custom_call_target="tpu_custom_call" | custom-call | tf_op jit(solution)/shard_map/route/pallas_call | solution.py:629
  25.9 0.0 copy-start.4
  25.9 0.7 copy-done.9
  26.6 1.1 %copy-done = f32[3,16,32,128]{3,2,1,0:T(8,128)S(1)} copy-done((f32[3,16,32,128]{3,2,1,0:T(8,128)S(1)}, f32[3,16,32,128]{3,2,1,0:T(8,128)}, u32[]{:S(2)}) %copy-start) | copy-done | bytes 786456
  27.7 1.1 %copy-done.2 = f32[3,16,32,128]{3,2,1,0:T(8,128)S(1)} copy-done((f32[3,16,32,128]{3,2,1,0:T(8,128)S(1)}, f32[3,16,32,128]{3,2,1,0:T(8,128)}, u32[]{:S(2)}) %copy-start.2) | copy-done | bytes 786456
  28.9 0.7 copy-done.5
  29.6 0.7 copy-done.6
  30.3 0.7 copy-done.7
  31.1 0.7 copy-done.8
  31.8 0.7 copy-done.10
  32.5 0.7 copy-done.11
  33.2 0.7 copy-done.12
  34.0 0.7 copy-done.13
  34.7 0.7 copy-done.14
  35.4 0.7 copy-done.15
  36.1 0.7 copy-done.16
  36.8 0.7 copy-done.17
  37.6 0.7 copy-done.18
  38.3 0.7 copy-done.19
  39.0 0.7 copy-done.20
  39.7 40.3 %climb_and_near.1 = (f32[640,128]{1,0:T(8,128)S(1)}, f32[320,128]{1,0:T(8,128)S(1)}, f32[160,128]{1,0:T(8,128)S(1)}, f32[80,128]{1,0:T(8,128)S(1)}, f32[160,128]...) custom-call(f32[3,16,32,128]{3,2,1,0:T(8,128)S(1)} %copy-done, ...), custom_call_target="tpu_custom_call" | custom-call | tf_op jit(solution)/shard_map/climb_and_near/pallas_call | solution.py:783
  80.0 0.1 pad_add_fusion.place_ref
  80.1 0.6 copy-done.21
  80.7 13.0 %descend.1 = f32[2,16,32,128]{3,2,1,0:T(8,128)} custom-call(s32[2]{0:T(128)S(1)} %pad_add_fusion.place_ref, f32[640,128]{1,0:T(8,128)S(1)} %get-tuple-element.55.refs_0_, f32[320,128]{1,0:T(8,128)S(1)} %get-tuple-element.56.refs_1_, f32[160,128]{1,0:T(8,128)S(1)} %get-tuple-element.57.refs_2_, f32[80,128]{1,0:T(8,128)S(1)} %get-tuple-element.58.refs_3_, ...), custom_call_target="tpu_custom_call" | custom-call | tf_op jit(solution)/shard_map/descend/pallas_call | solution.py:354
  (24 shorter events, 0.0 us)
Async XLA Ops:
  25.9 0.7 copy-start.9
  25.9 0.7 copy-start.4
  26.6 1.1 %copy-start = (f32[3,16,32,128]{3,2,1,0:T(8,128)S(1)}, f32[3,16,32,128]{3,2,1,0:T(8,128)}, u32[]{:S(2)}) copy-start(f32[3,16,32,128]{3,2,1,0:T(8,128)} %get-tuple-element.37.refs_0_.refs_17_) | copy-start | bytes 2359300
  27.7 1.1 %copy-start.2 = (f32[3,16,32,128]{3,2,1,0:T(8,128)S(1)}, f32[3,16,32,128]{3,2,1,0:T(8,128)}, u32[]{:S(2)}) copy-start(f32[3,16,32,128]{3,2,1,0:T(8,128)} %get-tuple-element.38.refs_1_) | copy-start | bytes 2359300
  28.9 0.7 copy-start.5
  29.6 0.7 copy-start.6
  30.3 0.7 copy-start.7
  31.1 0.7 copy-start.8
  31.8 0.7 copy-start.10
  32.5 0.7 copy-start.11
  33.2 0.7 copy-start.12
  34.0 0.7 copy-start.13
  34.7 0.7 copy-start.14
  35.4 0.7 copy-start.15
  36.1 0.7 copy-start.16
  36.8 0.7 copy-start.17
  37.6 0.7 copy-start.18
  38.3 0.7 copy-start.19
  39.0 0.7 copy-start.20
  39.7 40.4 %copy-start.1 = (f32[3,16,32,128]{3,2,1,0:T(8,128)S(1)}, f32[3,16,32,128]{3,2,1,0:T(8,128)}, u32[]{:S(2)}) copy-start(f32[3,16,32,128]{3,2,1,0:T(8,128)} %get-tuple-element.37.refs_0_.refs_17_) | copy-start | bytes 2359300
  39.7 40.4 %copy-start.3 = (bf16[160,888]{1,0:T(8,128)(2,1)S(1)}, bf16[160,888]{1,0:T(8,128)(2,1)}, u32[]{:S(2)}) copy-start(bf16[160,888]{1,0:T(8,128)(2,1)} %constant.16.clone.refs_13_) | copy-start | bytes 852484
  80.0 0.7 copy-start.21

commit v4 on v3

--- a/solution.py
+++ b/solution.py
@@ -452,12 +452,22 @@
 
 LANES = 128
 PER_CHUNK = 8
-
-
-def three_parts(value):
-    high = value.astype(jnp.bfloat16).astype(jnp.float32)
-    middle = (value - high).astype(jnp.bfloat16).astype(jnp.float32)
-    return [high, middle, (value - high) - middle]
+PARTS = 2
+
+
+def split_parts(value):
+    parts = []
+    for _ in range(PARTS):
+        parts.append(value.astype(jnp.bfloat16).astype(jnp.float32))
+        value = value - parts[-1]
+    return parts
+
+
+def joined_parts(acc_ref, v):
+    total = acc_ref[:, PARTS * v * LANES : (PARTS * v + 1) * LANES]
+    for p in range(PARTS * v + 1, PARTS * (v + 1)):
+        total = total + acc_ref[:, p * LANES : (p + 1) * LANES]
+    return total
 
 
 def one_hot_rows(index_row, rows):
@@ -497,7 +507,7 @@
         dest = dest + mask * (inside + above + float(o * CAP - 1))
     dest = dest.astype(jnp.int32)
     address = slot_ref[...] * leaves + leaf_ref[...]
-    parts = three_parts(pos_ref[0]) + three_parts(pos_ref[1]) + three_parts(strength_ref[...])
+    parts = split_parts(pos_ref[0]) + split_parts(pos_ref[1]) + split_parts(strength_ref[...])
     parts.append(((address >> 8) + 1).astype(jnp.float32))
     parts.append((address & 255).astype(jnp.float32))
     to_row, to_lane = dest >> 7, dest & 127
@@ -509,10 +519,10 @@
         acc_ref[...] = product if chunk == 0 else acc_ref[...] + product
     for v in range(4):
         if v < 3:
-            block = [acc_ref[:, (3 * v + p) * LANES : (3 * v + p + 1) * LANES] for p in range(3)]
-            value = (block[0] + block[1]) + block[2]
+            value = joined_parts(acc_ref, v)
         else:
-            value = (acc_ref[:, 9 * LANES : 10 * LANES] - 1.0) * 256.0 + acc_ref[:, 10 * LANES :]
+            tail = 3 * PARTS * LANES
+            value = (acc_ref[:, tail : tail + LANES] - 1.0) * 256.0 + acc_ref[:, tail + LANES :]
         for c in range(cells):
             packed_ref[c, v * 8 : (v + 1) * 8, :] = value[c * 8 : (c + 1) * 8]
 
@@ -522,7 +532,7 @@
     to_row, to_lane = place >> 7, place & 127
     parts = []
     for v in range(3):
-        parts += three_parts(arrived[v * 8 : (v + 1) * 8, :])
+        parts += split_parts(arrived[v * 8 : (v + 1) * 8, :])
     parts.append(jnp.ones_like(parts[0]))
     for j in range(PER_CHUNK):
         row = slice(j, j + 1)
@@ -533,13 +543,12 @@
 def finish_settle(pos_ref, strength_ref, out_ref, first_ref, last_ref, pack_ref, acc_ref):
     half_slots, cells_y, cells_x = strength_ref.shape
     rows = half_slots * cells_y
-    taken = acc_ref[:, 9 * LANES :] > 0.5
+    taken = acc_ref[:, 3 * PARTS * LANES :] > 0.5
     packed = jnp.zeros(pack_ref.shape, jnp.float32)
     which = lax.broadcasted_iota(jnp.int32, (8, cells_x), 0)
     for v in range(3):
-        block = [acc_ref[:, (3 * v + p) * LANES : (3 * v + p + 1) * LANES] for p in range(3)]
         old = (strength_ref[...] if v == 2 else pos_ref[v]).reshape(rows, cells_x)
-        value = jnp.where(taken, (block[0] + block[1]) + block[2], old)
+        value = jnp.where(taken, joined_parts(acc_ref, v), old)
         out_ref[v] = value.reshape(half_slots, cells_y, cells_x)
         pick = (lanes_of((8, cells_x)) == side_lane(which, v, cells_x)).astype(jnp.float32)
         packed = packed + lax.dot_general(pick, value, (((1,), (1,)), ((), ())), **HIGH)
@@ -556,105 +565,6 @@
     for rep in (0, 1):
         offsets += [(0, -1, rep), (0, 1, rep)] + [(c, l, rep) for c, l in AROUND]
     return offsets
-
-
-def route_kernel(*refs, leaves, cells, levels):
-    inputs, refs = refs[:7], refs[7:]
-    own_ref, received, refs = refs[0], refs[1:18], refs[18:]
-    held, refs = refs[:7], refs[7:]
-    (
-        packed_ref, arrived_ref, a_pack, b_pack, acc_pack, a_ref, b_ref, acc_ref,
-        first_ref, last_ref, side_ref, load_sem, move_send, move_recv, send_sem, recv_sem,
-    ) = refs
-    offsets = particle_offsets()
-    partners = [(None, turned((i, 0), cells, levels, 1)) for i in range(1, cells)]
-    partners += [position(o, cells, levels, 1) for o in offsets if o[1] or o[2]]
-    all_in = greet(partners)
-    loads = [
-        pltpu.make_async_copy(source, target, load_sem.at[i])
-        for i, (source, target) in enumerate(zip(inputs, held))
-    ]
-    for load in loads:
-        load.start()
-    for load in loads[:5]:
-        load.wait()
-    pos_ref, strength_ref = held[5:]
-    pack_into(packed_ref, *held[:5], a_pack, b_pack, acc_pack, leaves)
-    acc_ref[...] = jnp.zeros_like(acc_ref)
-    me = lax.axis_index("cell")
-    all_in()
-
-    def move(i):
-        target = turned((i, 0), cells, levels, 1)
-        return pltpu.make_async_remote_copy(
-            src_ref=packed_ref.at[target[0]],
-            dst_ref=arrived_ref.at[i],
-            send_sem=move_send.at[i],
-            recv_sem=move_recv.at[i],
-            device_id=target,
-            device_id_type=MESH,
-        )
-
-    for i in range(1, cells):
-        move(i).start()
-    arrived_ref[0] = packed_ref[me]
-    settle_chunk(arrived_ref[0], a_ref, b_ref, acc_ref)
-
-    def one_source(i, carry):
-        move(i).wait_recv()
-        settle_chunk(arrived_ref[i], a_ref, b_ref, acc_ref)
-        return carry
-
-    lax.fori_loop(1, cells, one_source, 0)
-    for load in loads[5:]:
-        load.wait()
-    finish_settle(pos_ref, strength_ref, own_ref, first_ref, last_ref, side_ref, acc_ref)
-    sources = [own_ref] + [last_ref, first_ref] + [side_ref] * 6 + [last_ref, first_ref] + [side_ref] * 6
-    swap = Exchange(sources, received, offsets, send_sem, recv_sem, cells, levels)
-    swap.start()
-    for i in range(1, cells):
-        move(i).wait_send()
-    swap.wait()
-
-
-def route(movers, pos, strength):
-    cells, levels = lax.axis_size("cell"), lax.axis_size("level")
-    half_slots, cells_y, cells_x = strength.shape
-    rows = half_slots * cells_y
-    own = (3,) + strength.shape
-    edge, side = (3 * half_slots, cells_x), (8, rows)
-    shapes = [own, own] + ([edge] * 2 + [side] * 6) * 2
-    inputs = list(movers) + [pos, strength]
-    wide = PER_CHUNK * LANES
-    return pl.pallas_call(
-        functools.partial(route_kernel, leaves=cells_y * cells_x, cells=cells, levels=levels),
-        out_shape=[jax.ShapeDtypeStruct(s, jnp.float32) for s in shapes],
-        in_specs=[pl.BlockSpec(memory_space=pl.ANY)] * len(inputs),
-        out_specs=[VMEM] * len(shapes),
-        scratch_shapes=[pltpu.VMEM(x.shape, x.dtype) for x in inputs]
-        + [
-            pltpu.VMEM((cells, 32, LANES), jnp.float32),
-            pltpu.VMEM((cells, 32, LANES), jnp.float32),
-            pltpu.VMEM((cells * 8, wide), jnp.bfloat16),
-            pltpu.VMEM((11 * LANES, wide), jnp.bfloat16),
-            pltpu.VMEM((cells * 8, 11 * LANES), jnp.float32),
-            pltpu.VMEM((rows, wide), jnp.bfloat16),
-            pltpu.VMEM((10 * LANES, wide), jnp.bfloat16),
-            pltpu.VMEM((rows, 10 * LANES), jnp.float32),
-            pltpu.VMEM(edge, jnp.float32),
-            pltpu.VMEM(edge, jnp.float32),
-            pltpu.VMEM(side, jnp.float32),
-            pltpu.SemaphoreType.DMA((7,)),
-            pltpu.SemaphoreType.DMA((cells,)),
-            pltpu.SemaphoreType.DMA((cells,)),
-            pltpu.SemaphoreType.DMA((17,)),
-            pltpu.SemaphoreType.DMA((17,)),
-        ],
-        compiler_params=pltpu.CompilerParams(
-            collective_id=0, has_side_effects=True, vmem_limit_bytes=56 * 1024 * 1024
-        ),
-        name="route",
-    )(*inputs)
 
 
 def side_lane(which, v, cells_x):
@@ -707,13 +617,18 @@
                     source_x = src_ref[step_x + 1, 0, s, there, :]
                     source_y = src_ref[step_x + 1, 1, s, there, :] + float(step_y)
                     strength = src_ref[step_x + 1, 2, s, there, :]
-                    for t in range(GROUP):
-                        gap_x = target_x[t] - source_x
-                        gap_y = target_y[t] - source_y
-                        square = gap_x * gap_x + (gap_y * gap_y + blob_square)
-                        weight = strength * pl.reciprocal(square, approx=True)
-                        sums[t] = sums[t] + weight * gap_x
-                        sums[GROUP + t] = sums[GROUP + t] + weight * gap_y
+                    for t in range(0, GROUP, 2):
+                        gaps, squares = [], []
+                        for u in (t, t + 1):
+                            gap_x = target_x[u] - source_x
+                            gap_y = target_y[u] - source_y
+                            gaps.append((gap_x, gap_y))
+                            squares.append(gap_x * gap_x + (gap_y * gap_y + blob_square))
+                        shared = strength * pl.reciprocal(squares[0] * squares[1], approx=True)
+                        for u, square, (gap_x, gap_y) in zip((t, t + 1), squares[::-1], gaps):
+                            weight = shared * square
+                            sums[u] = sums[u] + weight * gap_x
+                            sums[GROUP + u] = sums[GROUP + u] + weight * gap_y
             return tuple(sums)
 
         zero = jnp.zeros((BAND, cells_x), jnp.float32)
@@ -726,25 +641,77 @@
     lax.fori_loop(0, (cells_y // BAND) * (half_slots // GROUP), one_block, 0)
 
 
-def climb_kernel(*refs, cells, levels):
-    own_ref, other_ref, refs = refs[0], refs[1], refs[2:]
-    frames, refs = [refs[:8], refs[8:16]], refs[16:]
-    up_ref, refs = refs[0], refs[1:]
-    owned, refs = refs[:HALO_LEVELS], refs[HALO_LEVELS:]
+def near_kernel(*refs, leaves, cells, levels):
+    inputs, up_ref, refs = refs[:7], refs[7], refs[8:]
+    own_ref, owned, refs = refs[0], refs[1 : 1 + HALO_LEVELS], refs[1 + HALO_LEVELS :]
     received, coarse_ref, near_ref, refs = refs[:8], refs[8], refs[9], refs[10:]
-    mine_ref, edges_ref, top_ref, low_ref, src_ref = refs[:5]
-    send_sem, recv_sem, coarse_send, coarse_recv = refs[5:]
+    held, particles, refs = refs[:7], refs[7:24], refs[24:]
+    (
+        packed_ref, arrived_ref, a_pack, b_pack, acc_pack, a_ref, b_ref, acc_ref,
+        first_ref, last_ref, side_ref, load_sem, move_send, move_recv, send_sem, recv_sem,
+    ) = refs[:16]
+    mine_ref, edges_ref, top_ref, low_ref, src_ref = refs[16:21]
+    level_send, level_recv, coarse_send, coarse_recv = refs[21:]
+    offsets = particle_offsets()
     turns = [(i, j) for i in range(cells) for j in range(levels) if i or j]
-    all_in = greet([(None, turned(turn, cells, levels, 1)) for turn in turns])
-    climb_into(own_ref, other_ref, up_ref, *owned, mine_ref, edges_ref)
+    partners = [(None, turned(turn, cells, levels, 1)) for turn in turns]
+    partners += [position(o, cells, levels, 1) for o in offsets if o[2]]
+    all_in = greet(partners)
+    loads = [
+        pltpu.make_async_copy(source, target, load_sem.at[i])
+        for i, (source, target) in enumerate(zip(inputs, held))
+    ]
+    for load in loads:
+        load.start()
+    for load in loads[:5]:
+        load.wait()
+    pos_ref, strength_ref = held[5:]
+    pack_into(packed_ref, *held[:5], a_pack, b_pack, acc_pack, leaves)
+    acc_ref[...] = jnp.zeros_like(acc_ref)
+    me = lax.axis_index("cell")
+    all_in()
+
+    def move(i):
+        target = turned((i, 0), cells, levels, 1)
+        return pltpu.make_async_remote_copy(
+            src_ref=packed_ref.at[target[0]],
+            dst_ref=arrived_ref.at[i],
+            send_sem=move_send.at[i],
+            recv_sem=move_recv.at[i],
+            device_id=target,
+            device_id_type=MESH,
+        )
+
+    for i in range(1, cells):
+        move(i).start()
+    arrived_ref[0] = packed_ref[me]
+    settle_chunk(arrived_ref[0], a_ref, b_ref, acc_ref)
+
+    def one_source(i, carry):
+        move(i).wait_recv()
+        settle_chunk(arrived_ref[i], a_ref, b_ref, acc_ref)
+        return carry
+
+    lax.fori_loop(1, cells, one_source, 0)
+    for load in loads[5:]:
+        load.wait()
+    finish_settle(pos_ref, strength_ref, own_ref, first_ref, last_ref, side_ref, acc_ref)
+    sources = [own_ref] + [last_ref, first_ref] + [side_ref] * 6 + [last_ref, first_ref] + [side_ref] * 6
+    swap = Exchange(sources, particles, offsets, send_sem, recv_sem, cells, levels)
+    swap.start()
+    for i in range(1, cells):
+        move(i).wait_send()
+    swap.wait()
+    climb_into(own_ref, particles[0], up_ref, *owned, mine_ref, edges_ref)
     edge = 2 * CHANNELS
     for k in range(HALO_LEVELS):
         here = slice(k * edge, (k + 1) * edge)
         top_ref[here, :] = owned[k][:edge, :]
         low_ref[here, :] = owned[k][owned[k].shape[0] - edge :, :]
+    frames = [particles[1:9], particles[9:17]]
     offsets = [(0, -1, 0), (0, 1, 0)] + [(c, l, 0) for c, l in AROUND]
     sources = [low_ref, top_ref] + [edges_ref] * 6
-    swap = Exchange(sources, received, offsets, send_sem, recv_sem, cells, levels)
+    swap = Exchange(sources, received, offsets, level_send, level_recv, cells, levels)
     rows = mine_ref.shape[0]
 
     def copy(i, source, target):
@@ -758,49 +725,73 @@
         )
 
     me = turned((0, 0), cells, levels, 1)
-    all_in()
     swap.start()
     for i, turn in enumerate(turns):
         copy(i, me, turned(turn, cells, levels, 1)).start()
     coarse_ref[me[0], pl.ds(pl.multiple_of(me[1] * rows, 8), rows), :] = mine_ref[...]
-    near_into(near_ref, own_ref, other_ref, frames, src_ref)
+    near_into(near_ref, own_ref, particles[0], frames, src_ref)
     swap.wait()
     for i, turn in enumerate(turns):
         copy(i, me, turned(turn, cells, levels, 1)).wait_send()
         copy(i, turned(turn, cells, levels, -1), me).wait_recv()
 
 
-def climb_and_near(own, other, frames):
+def route_and_near(movers, pos, strength):
     cells, levels = lax.axis_size("cell"), lax.axis_size("level")
-    half_slots, cells_y, cells_x = own.shape[1:]
+    half_slots, cells_y, cells_x = strength.shape
+    slot_rows = half_slots * cells_y
+    own = (3,) + strength.shape
+    edge, side = (3 * half_slots, cells_x), (8, slot_rows)
+    particles = [own] + ([edge] * 2 + [side] * 6) * 2
     owned = [(CHANNELS * (cells_y >> k), cells_x) for k in range(HALO_LEVELS)]
     mine = (CHANNELS * (cells_y >> HALO_LEVELS), cells_x)
     edges = (8, pack_starts(cells_y)[-1])
     rows = (2 * CHANNELS * HALO_LEVELS, cells_x)
-    shapes = owned + [rows] * 2 + [edges] * 6
-    shapes += [(cells, levels * mine[0], cells_x), (2,) + own.shape[1:]]
-    inputs = [own, other, *frames, jnp.asarray(upward_matrix())]
+    shapes = [own] + owned + [rows] * 2 + [edges] * 6
+    shapes += [(cells, levels * mine[0], cells_x), (2,) + strength.shape]
+    inputs = list(movers) + [pos, strength]
+    wide = PER_CHUNK * LANES
+    floats = lambda *shape: pltpu.VMEM(shape, jnp.float32)
+    halves = lambda *shape: pltpu.VMEM(shape, jnp.bfloat16)
     return pl.pallas_call(
-        functools.partial(climb_kernel, cells=cells, levels=levels),
+        functools.partial(near_kernel, leaves=cells_y * cells_x, cells=cells, levels=levels),
         out_shape=[jax.ShapeDtypeStruct(s, jnp.float32) for s in shapes],
-        in_specs=[VMEM] * len(inputs),
+        in_specs=[pl.BlockSpec(memory_space=pl.ANY)] * len(inputs) + [VMEM],
         out_specs=[VMEM] * len(shapes),
-        scratch_shapes=[
-            pltpu.VMEM(mine, jnp.float32),
-            pltpu.VMEM(edges, jnp.float32),
-            pltpu.VMEM(rows, jnp.float32),
-            pltpu.VMEM(rows, jnp.float32),
-            pltpu.VMEM((3, 3, 2 * half_slots, cells_y + 2 * FRONT, cells_x), jnp.float32),
+        scratch_shapes=[pltpu.VMEM(x.shape, x.dtype) for x in inputs]
+        + [floats(*shape) for shape in particles]
+        + [
+            floats(cells, 32, LANES),
+            floats(cells, 32, LANES),
+            halves(cells * 8, wide),
+            halves((3 * PARTS + 2) * LANES, wide),
+            floats(cells * 8, (3 * PARTS + 2) * LANES),
+            halves(slot_rows, wide),
+            halves((3 * PARTS + 1) * LANES, wide),
+            floats(slot_rows, (3 * PARTS + 1) * LANES),
+            floats(*edge),
+            floats(*edge),
+            floats(*side),
+            pltpu.SemaphoreType.DMA((7,)),
+            pltpu.SemaphoreType.DMA((cells,)),
+            pltpu.SemaphoreType.DMA((cells,)),
+            pltpu.SemaphoreType.DMA((17,)),
+            pltpu.SemaphoreType.DMA((17,)),
+            floats(*mine),
+            floats(*edges),
+            floats(*rows),
+            floats(*rows),
+            floats(3, 3, 2 * half_slots, cells_y + 2 * FRONT, cells_x),
             pltpu.SemaphoreType.DMA((8,)),
             pltpu.SemaphoreType.DMA((8,)),
             pltpu.SemaphoreType.DMA((cells * levels - 1,)),
             pltpu.SemaphoreType.DMA((cells * levels - 1,)),
         ],
         compiler_params=pltpu.CompilerParams(
-            collective_id=1, has_side_effects=True, vmem_limit_bytes=48 * 1024 * 1024
+            collective_id=0, has_side_effects=True, vmem_limit_bytes=48 * 1024 * 1024
         ),
-        name="climb_and_near",
-    )(*inputs)
+        name="route_and_near",
+    )(*inputs, jnp.asarray(upward_matrix()))
 
 
 def local(
@@ -816,8 +807,7 @@
         mover_leaf.reshape(-1, LANES),
         mover_slot.reshape(-1, LANES),
     ]
-    own, other, *frames = route(movers, resident_pos, resident_strength)
-    got = climb_and_near(own, other, frames)
+    own, *got = route_and_near(movers, resident_pos, resident_strength)
     owned, got = got[:HALO_LEVELS], got[HALO_LEVELS:]
     return descend(
         place, owned, got[:8], got[8], got[9], own, cells * (cells_x >> HALO_LEVELS)

time: 95.1 us -> 83.2 us (0.87)
  local copies, waits for them, and re-layouts: 14.4 us -> 6.24 us
  Pallas kernels: 79.2 us -> 76.3 us
    unnamed x44 -> x20, local copies, waits for them, and re-layouts: 14.4 us -> 6.24 us
    pallas_call x2 -> x1, Pallas kernels: 66.1 us -> 63.1 us  [route_and_near(): pl.pallas_call(functools.partial(near_kernel, leaves=cells_y * cells_x, c...]
where the time goes in v4:
time: 83.2 us; the launch traced here: 82.7 us
  Pallas kernels  76.3 us (92%)
  local copies, waits for them, and re-layouts  6.24 us (8%)
    pallas_call x1, Pallas kernels, route_and_near(): pl.pallas_call(functools.partial(near_kernel, leaves=cells_y * cells_x, c...  63.1 us
    pallas_call x1, Pallas kernels, descend(): pl.pallas_call(functools.partial(downward_kernel, cells_y=cells_y, cells_...  13.2 us
    unnamed x20, local copies, waits for them, and re-layouts  6.24 us

profile of v4, /device:TPU:0, one launch (start us, length us, event | category | flops | bytes accessed | tf_op | source)
XLA Modules:
  0.0 82.7 jit_solution(12183456237923271991)
XLA Ops:
  0.0 0.0 copy-start.5
  0.0 0.0 copy-start.3
  0.0 0.1 pad_add_fusion.place_ref
  0.1 0.6 copy-done.5
  0.7 0.0 copy-done.3
  0.7 0.0 copy-start
  0.7 1.0 %copy-done = f32[2,16,32,128]{3,2,1,0:T(8,128)S(1)} copy-done((f32[2,16,32,128]{3,2,1,0:T(8,128)S(1)}, f32[2,16,32,128]{3,2,1,0:T(8,128)}, u32[]{:S(2)}) %copy-start) | copy-done | bytes 524312
  1.8 0.0 copy-start.2
  1.8 0.9 %copy-done.2 = f32[16,32,128]{2,1,0:T(8,128)S(1)} copy-done((f32[16,32,128]{2,1,0:T(8,128)S(1)}, f32[16,32,128]{2,1,0:T(8,128)}, u32[]{:S(2)}) %copy-start.2) | copy-done | bytes 262168
  2.7 0.0 copy-start.4
  2.7 0.8 copy-done.4
  3.5 0.0 copy-start.6
  3.5 0.7 copy-done.6
  4.2 0.0 copy-start.7
  4.2 0.7 copy-done.7
  4.9 0.0 copy-start.8
  4.9 0.7 copy-done.8
  5.6 0.0 copy-start.1
  5.6 63.1 %route_and_near.1 = (f32[3,16,32,128]{3,2,1,0:T(8,128)S(1)}, f32[640,128]{1,0:T(8,128)S(1)}, f32[320,128]{1,0:T(8,128)S(1)}, f32[160,128]{1,0:T(8,128)S(1)}, f32...) custom-call(f32[2,32,128]{2,1,0:T(8,128)S(1)} %bitcast.7, ...), custom_call_target="tpu_custom_call" | custom-call | tf_op jit(solution)/shard_map/route_and_near/pallas_call | solution.py:756
  68.8 0.0 copy-start.9
  68.8 0.0 copy-done.1
  68.8 0.7 copy-done.9
  69.5 13.2 %descend.1 = f32[2,16,32,128]{3,2,1,0:T(8,128)} custom-call(s32[2]{0:T(128)S(1)} %pad_add_fusion.place_ref, f32[640,128]{1,0:T(8,128)S(1)} %get-tuple-element.20.refs_0_, f32[320,128]{1,0:T(8,128)S(1)} %get-tuple-element.21.refs_1_, f32[160,128]{1,0:T(8,128)S(1)} %get-tuple-element.22.refs_2_, f32[80,128]{1,0:T(8,128)S(1)} %get-tuple-element.23.refs_3_, ...), custom_call_target="tpu_custom_call" | custom-call | tf_op jit(solution)/shard_map/descend/pallas_call | solution.py:354
Async XLA Ops:
  0.0 0.7 copy-start.5
  0.0 0.7 copy-start.3
  0.7 1.0 %copy-start = (f32[2,16,32,128]{3,2,1,0:T(8,128)S(1)}, f32[2,16,32,128]{3,2,1,0:T(8,128)}, u32[]{:S(2)}) copy-start(f32[2,16,32,128]{3,2,1,0:T(8,128)} %refs_5_.1) | copy-start | bytes 1572868
  1.8 0.9 %copy-start.2 = (f32[16,32,128]{2,1,0:T(8,128)S(1)}, f32[16,32,128]{2,1,0:T(8,128)}, u32[]{:S(2)}) copy-start(f32[16,32,128]{2,1,0:T(8,128)} %refs_6_.1) | copy-start | bytes 786436
  2.7 0.8 copy-start.4
  3.5 0.7 copy-start.6
  4.2 0.7 copy-start.7
  4.9 0.7 copy-start.8
  5.6 63.2 %copy-start.1 = (bf16[160,888]{1,0:T(8,128)(2,1)S(1)}, bf16[160,888]{1,0:T(8,128)(2,1)}, u32[]{:S(2)}) copy-start(bf16[160,888]{1,0:T(8,128)(2,1)} %constant.16.clone.refs_13_) | copy-start | bytes 852484
  68.8 0.7 copy-start.9

commit v5 on v4

--- a/solution.py
+++ b/solution.py
@@ -617,18 +617,13 @@
                     source_x = src_ref[step_x + 1, 0, s, there, :]
                     source_y = src_ref[step_x + 1, 1, s, there, :] + float(step_y)
                     strength = src_ref[step_x + 1, 2, s, there, :]
-                    for t in range(0, GROUP, 2):
-                        gaps, squares = [], []
-                        for u in (t, t + 1):
-                            gap_x = target_x[u] - source_x
-                            gap_y = target_y[u] - source_y
-                            gaps.append((gap_x, gap_y))
-                            squares.append(gap_x * gap_x + (gap_y * gap_y + blob_square))
-                        shared = strength * pl.reciprocal(squares[0] * squares[1], approx=True)
-                        for u, square, (gap_x, gap_y) in zip((t, t + 1), squares[::-1], gaps):
-                            weight = shared * square
-                            sums[u] = sums[u] + weight * gap_x
-                            sums[GROUP + u] = sums[GROUP + u] + weight * gap_y
+                    for t in range(GROUP):
+                        gap_x = target_x[t] - source_x
+                        gap_y = target_y[t] - source_y
+                        square = gap_x * gap_x + (gap_y * gap_y + blob_square)
+                        weight = strength * pl.reciprocal(square, approx=True)
+                        sums[t] = sums[t] + weight * gap_x
+                        sums[GROUP + t] = sums[GROUP + t] + weight * gap_y
             return tuple(sums)
 
         zero = jnp.zeros((BAND, cells_x), jnp.float32)

time: 83.2 us -> 81.2 us (0.976)
  Pallas kernels: 76.3 us -> 74.2 us
    pallas_call x1, Pallas kernels: 63.1 us -> 61.1 us  [route_and_near(): pl.pallas_call(functools.partial(near_kernel, leaves=cells_y * cells_x, c...]
where the time goes in v5:
time: 81.2 us; the launch traced here: 80.6 us
  Pallas kernels  74.2 us (91%)
  local copies, waits for them, and re-layouts  6.24 us (8%)
    pallas_call x1, Pallas kernels, route_and_near(): pl.pallas_call(functools.partial(near_kernel, leaves=cells_y * cells_x, c...  61.1 us
    pallas_call x1, Pallas kernels, descend(): pl.pallas_call(functools.partial(downward_kernel, cells_y=cells_y, cells_...  13.2 us
    unnamed x20, local copies, waits for them, and re-layouts  6.24 us

profile of v5, /device:TPU:0, one launch (start us, length us, event | category | flops | bytes accessed | tf_op | source)
XLA Modules:
  0.0 80.6 jit_solution(12826960963054452855)
XLA Ops:
  0.0 0.0 copy-start.5
  0.0 0.0 copy-start.3
  0.0 0.1 pad_add_fusion.place_ref
  0.1 0.6 copy-done.5
  0.7 0.0 copy-done.3
  0.7 0.0 copy-start
  0.7 1.0 %copy-done = f32[2,16,32,128]{3,2,1,0:T(8,128)S(1)} copy-done((f32[2,16,32,128]{3,2,1,0:T(8,128)S(1)}, f32[2,16,32,128]{3,2,1,0:T(8,128)}, u32[]{:S(2)}) %copy-start) | copy-done | bytes 524312
  1.8 0.0 copy-start.2
  1.8 0.9 %copy-done.2 = f32[16,32,128]{2,1,0:T(8,128)S(1)} copy-done((f32[16,32,128]{2,1,0:T(8,128)S(1)}, f32[16,32,128]{2,1,0:T(8,128)}, u32[]{:S(2)}) %copy-start.2) | copy-done | bytes 262168
  2.7 0.0 copy-start.4
  2.7 0.8 copy-done.4
  3.5 0.0 copy-start.6
  3.5 0.7 copy-done.6
  4.2 0.0 copy-start.7
  4.2 0.7 copy-done.7
  4.9 0.0 copy-start.8
  4.9 0.7 copy-done.8
  5.6 0.0 copy-start.1
  5.6 61.1 %route_and_near.1 = (f32[3,16,32,128]{3,2,1,0:T(8,128)S(1)}, f32[640,128]{1,0:T(8,128)S(1)}, f32[320,128]{1,0:T(8,128)S(1)}, f32[160,128]{1,0:T(8,128)S(1)}, f32...) custom-call(f32[2,32,128]{2,1,0:T(8,128)S(1)} %bitcast.7, ...), custom_call_target="tpu_custom_call" | custom-call | tf_op jit(solution)/shard_map/route_and_near/pallas_call | solution.py:751
  66.7 0.0 copy-start.9
  66.7 0.0 copy-done.1
  66.7 0.7 copy-done.9
  67.4 13.2 %descend.1 = f32[2,16,32,128]{3,2,1,0:T(8,128)} custom-call(s32[2]{0:T(128)S(1)} %pad_add_fusion.place_ref, f32[640,128]{1,0:T(8,128)S(1)} %get-tuple-element.20.refs_0_, f32[320,128]{1,0:T(8,128)S(1)} %get-tuple-element.21.refs_1_, f32[160,128]{1,0:T(8,128)S(1)} %get-tuple-element.22.refs_2_, f32[80,128]{1,0:T(8,128)S(1)} %get-tuple-element.23.refs_3_, ...), custom_call_target="tpu_custom_call" | custom-call | tf_op jit(solution)/shard_map/descend/pallas_call | solution.py:354
Async XLA Ops:
  0.0 0.7 copy-start.5
  0.0 0.7 copy-start.3
  0.7 1.0 %copy-start = (f32[2,16,32,128]{3,2,1,0:T(8,128)S(1)}, f32[2,16,32,128]{3,2,1,0:T(8,128)}, u32[]{:S(2)}) copy-start(f32[2,16,32,128]{3,2,1,0:T(8,128)} %refs_5_.1) | copy-start | bytes 1572868
  1.8 0.9 %copy-start.2 = (f32[16,32,128]{2,1,0:T(8,128)S(1)}, f32[16,32,128]{2,1,0:T(8,128)}, u32[]{:S(2)}) copy-start(f32[16,32,128]{2,1,0:T(8,128)} %refs_6_.1) | copy-start | bytes 786436
  2.7 0.8 copy-start.4
  3.5 0.7 copy-start.6
  4.2 0.7 copy-start.7
  4.9 0.7 copy-start.8
  5.6 61.1 %copy-start.1 = (bf16[160,888]{1,0:T(8,128)(2,1)S(1)}, bf16[160,888]{1,0:T(8,128)(2,1)}, u32[]{:S(2)}) copy-start(bf16[160,888]{1,0:T(8,128)(2,1)} %constant.16.clone.refs_13_) | copy-start | bytes 852484
  66.7 0.7 copy-start.9
